TPU v7x, 32 devices: a whole 2x2x4 slice. The times are simulated.
32 devices in a mesh: row: 8 (over y, x, core), col: 4 (over z).
Axes of the slice: x: 2, y: 2, z: 4, core: 2. Of those that a mesh axis runs over, the one named last changes fastest.
Arguments:
- amplitudes: float32 [65536, 256], P(None, ('row', 'col')), may hold values from -6 to 6
- integrals: float32 [5632, 65536], P('row', 'col'), may hold values from -0.0234375 to 0.0234375
Outputs:
- ladder: float32 [5632, 256], P('row', 'col')
All inputs are finite; a program needn't handle non-finite values.
Results may differ from a plain program's by a relative error of at most 0.00007.
Values sent between devices are 32-bit elements; how exact they have to be, the bound alone decides.
No kernel may reach another device: no remote copies, remote signals or barrier semaphores. Data moves between devices by JAX's collectives and lax.ppermute only.
A program may use at most 128 MiB of HBM per device.

v0:
```python
import jax
import jax.numpy as jnp
from jax import lax
from jax.sharding import PartitionSpec as P


def per_device(amplitudes, integrals):
    cd_panel = lax.all_to_all(amplitudes, "col", split_axis=0, concat_axis=1, tiled=True)
    partial_value = jnp.dot(
        integrals,
        lax.all_gather(cd_panel, "row", axis=1, tiled=True),
        preferred_element_type=jnp.float32,
        precision=lax.Precision.HIGHEST,
    )
    contracted = lax.psum_scatter(partial_value, "col", scatter_dimension=1, tiled=True)
    return 0.5 * contracted


def solution(mesh):
    return jax.shard_map(
        per_device,
        mesh=mesh,
        in_specs=(P(None, ("row", "col")), P("row", "col")),
        out_specs=P("row", "col"),
        check_vma=False,
    )
```

profile of v0, /device:TPU:0, one launch (start us, length us, event | category | flops | bytes accessed | tf_op | source)
XLA Modules:
  0.0 233.6 jit_solution(15858017224405565455)
XLA Ops:
  6.5 0.0 all-gather.2.cloned.1.call-start
  6.5 54.6 %all_to_all.19 = f32[4,16384,8]{1,2,0:T(8,128)} all-to-all(f32[4,16384,8]{1,2,0:T(8,128)} %bitcast.7), channel_id=1, replica_groups=mesh['row'=8,'col'=4] {'col'}, dimensions={0} | all-to-all | bytes 4194304 | tf_op jit(solution)/shard_map/all_to_all | solution.py:8
  61.2 0.0 all-gather.2.cloned.1.call-update
  61.2 0.0 reduce-scatter.2.cloned.1.call-start
  61.2 89.2 %all-gather.2.cloned.1.call-done = f32[16384,256]{0,1:T(8,128)} async-done(((f32[16384,32]{0,1:T(8,128)}), f32[16384,256]{0,1:T(8,128)}) %all-gather.2.cloned.1.call-update) | async-done | bytes 16777232 | tf_op jit(solution)/shard_map/all_gather | solution.py:11
  150.4 51.3 %fusion = f32[704,256]{0,1:T(8,128)} fusion(f32[704,16384]{1,0:T(8,128)} %param.3, f32[16384,256]{0,1:T(8,128)} %all-gather.2.cloned.1.call-done), kind=kOutput, calls=%fused_computation.1 | convolution fusion | flops 35433480192 | bytes 63635456 | tf_op jit(solution)/shard_map/dot_general | solution.py:9
  201.7 0.0 reduce-scatter.2.cloned.1.call-update
  201.7 23.4 %reduce-scatter.2.cloned.1.call-done = f32[704,64]{0,1:T(8,128)} async-done(((f32[704,256]{0,1:T(8,128)}), f32[704,64]{0,1:T(8,128)}) %reduce-scatter.2.cloned.1.call-update) | async-done | bytes 180240 | tf_op jit(solution)/shard_map/reduce_scatter | solution.py:15
  225.2 1.6 broadcast_multiply_fusion
Async XLA Ops:
  6.5 143.9 %all-gather.2.cloned.1.call-start = ((), (), s32[]{:S(2)}) async-start(), calls=%async_computation.2 | async-start | bytes 18874368 | tf_op jit(solution)/shard_map/all_gather | solution.py:11
  61.2 164.0 %reduce-scatter.2.cloned.1.call-start = ((), (), s32[]{:S(2)}) async-start(), calls=%async_computation.3 | async-start | bytes 983040 | tf_op jit(solution)/shard_map/reduce_scatter | solution.py:15
Sparse Core Ops, SparseCore 0:
  61.3 89.0 all-gather.1
  201.9 23.2 reduce-scatter.1
where the time goes:
time: 234 us
  waiting for transfers between devices  113 us (48%)
  blocking collectives  54.6 us (23%)
  matrix products  51.3 us (22%)
  between operations  13.4 us (6%)
    all_gather x1, waiting for transfers between devices, per_device(): lax.all_gather(cd_panel, 'row', axis=1, tiled=True)  89.2 us
    all_to_all x1, blocking collectives, per_device(): lax.all_to_all(amplitudes, 'col', split_axis=0, concat_axis=1, tiled=True)  54.6 us
    dot_general x1, matrix products, per_device(): jnp.dot(integrals, lax.all_gather(cd_panel, 'row', axis=1, tiled=True), p...  51.3 us
    reduce_scatter x1, waiting for transfers between devices, per_device(): lax.psum_scatter(partial_value, 'col', scatter_dimension=1, tiled=True)  23.4 us
  transfers between devices with their start and end apart: 2, of which 2 were waited for; matrix products, arithmetic and copies ran while one was open for 0% of the time, Pallas kernels for 0%

commit v1 on v0

v1 whole, which is shorter than its diff:
```python
import functools

import jax
import jax.numpy as jnp
from jax import lax
from jax.experimental import pallas as pl
from jax.experimental.pallas import tpu as pltpu
from jax.sharding import PartitionSpec as P

F32, BF16 = jnp.float32, jnp.bfloat16
NT = (((1,), (1,)), ((), ()))
SUB, LANE = 8, 128

PARTS = (3, 3, 2)
TILE, LIMIT = 2048, 28
COST = 3


def split(x):
    hi = x.astype(BF16)
    return hi, (x - hi.astype(F32)).astype(BF16)


def product(v, t):
    dot = lambda a, b: lax.dot_general(a, b, NT, preferred_element_type=F32)
    vh, vl = split(v)
    th, tl = split(t)
    return dot(vh, th) + (dot(vh, tl) + dot(vl, th))


def kernel(where, v_ref, *refs, groups, cols, lanes, acc, last):
    step = pl.program_id(0)
    if last:
        out_ref, tau, total = refs[-3:]
    else:
        out_ref, tau = refs[-2:]
        total = out_ref
    chip, core, col = where[0], where[1], where[2]
    for g, distances in enumerate(groups):
        for other in range(2):
            ref = refs[2 * g + other]
            its = core if other == 0 else 1 - core
            one, two = its + 1, 2 - its
            for m, source in enumerate((chip, chip ^ one, chip ^ two, chip ^ 3)):
                for k, d in enumerate(distances):
                    at = ((source * 2 + its) * cols + (col ^ d)) * lanes
                    tau[pl.ds(pl.multiple_of(at, lanes), lanes), :] = ref[pl.ds((m * len(distances) + k) * lanes, lanes), :]
    new = product(v_ref[...], tau[...])

    @pl.when(step == 0)
    def _():
        total[...] = new + refs[2 * len(groups)][...] if acc else new

    @pl.when(step > 0)
    def _():
        total[...] += new

    if last:

        @pl.when(step == pl.num_programs(0) - 1)
        def _():
            rows = total.shape[0]
            out_ref[:, :rows] = total[...].T
            if rows < out_ref.shape[1]:
                out_ref[:, rows:] = jnp.zeros((out_ref.shape[0], out_ref.shape[1] - rows), F32)


def multiply(where, v, quads, groups, acc, at, width, tile, cols, lanes, last):
    rows, ij = v.shape[0], 8 * lanes * cols
    whole = pl.BlockSpec((rows, ij), lambda i, w: (0, 0))
    specs, operands = [pl.BlockSpec((rows, tile), lambda i, w: (0, i + at // tile))], [v]
    for own, theirs, begin in quads:
        for a in (own, theirs):
            specs.append(pl.BlockSpec((a.shape[0], tile), lambda i, w, b=begin: (0, i + (at - b) // tile)))
            operands.append(a)
    if acc is not None:
        specs.append(whole)
        operands.append(acc)
    scratch = [pltpu.VMEM((ij, tile), F32)]
    if last:
        shape = (ij, pl.cdiv(rows, LANE) * LANE)
        spec = pl.BlockSpec(shape, lambda i, w: (0, 0))
        scratch.append(pltpu.VMEM((rows, ij), F32))
    else:
        shape, spec = (rows, ij), whole
    return pl.pallas_call(
        functools.partial(kernel, groups=groups, cols=cols, lanes=lanes, acc=acc is not None, last=last),
        grid_spec=pltpu.PrefetchScalarGridSpec(
            num_scalar_prefetch=1, grid=(width // tile,), in_specs=specs, out_specs=spec, scratch_shapes=scratch
        ),
        out_shape=jax.ShapeDtypeStruct(shape, F32),
        input_output_aliases={len(operands): 0} if acc is not None and not last else {},
        cost_estimate=pl.CostEstimate(
            flops=COST * 6 * rows * ij * width, bytes_accessed=COST * 4 * (rows + ij) * width, transcendentals=0
        ),
        compiler_params=pltpu.CompilerParams(vmem_limit_bytes=LIMIT << 20),
    )(where, *operands)


def xor(n, bits):
    return [(i, i ^ bits) for i in range(n)]


def pipelined(amplitudes, integrals):
    tau = amplitudes.T
    lanes, (height, block) = tau.shape[0], integrals.shape
    row, col = lax.axis_index("row"), lax.axis_index("col")
    rows, cols = lax.axis_size("row"), lax.axis_size("col")
    where = jnp.stack([row // 2, row % 2, col]).astype(jnp.int32)
    near = [(i, i ^ (2 if i % 2 == 0 else 4)) for i in range(rows)]
    far = [(i, i ^ (4 if i % 2 == 0 else 2)) for i in range(rows)]
    parts = [p * block // 8 for p in PARTS]
    begins = [sum(parts[:i]) for i in range(len(parts))]
    seen = []
    piece, first, both, quad, theirs, gone = {}, {}, {}, {}, {}, {}
    acc = None

    def send(x, axis, pairs):
        return lax.ppermute(lax.optimization_barrier((x, *seen))[0], axis, pairs)

    def cut(d, begin, width):
        return lax.dynamic_slice(tau, (0, (col ^ d) * block + begin), (lanes, width))

    def along(u):
        if u == 1:
            gone[u] = [send(cut(1, 0, block), "col", xor(cols, 1))]
        else:
            gone[u] = [send(cut(d, begins[u - 2], parts[u - 2]), "col", xor(cols, d)) for d in range(2, cols)]
        piece[u] = jnp.concatenate(gone[u], 0)

    def to_near(u):
        first[u] = send(piece[u], "row", near)

    def to_far(u):
        pair = jnp.concatenate([piece[u], first[u]], 0)
        both[u] = send(pair, "row", far)
        quad[u] = jnp.concatenate([pair, both[u]], 0)

    def swap(u):
        theirs[u] = send(quad[u], "row", xor(rows, 1))

    def multiply_part(u):
        nonlocal acc
        quads = [(quad[0], theirs[0], 0), (quad[1], theirs[1], 0), (quad[u], theirs[u], begins[u - 2])]
        groups = ((0,), (1,), tuple(range(2, cols)))
        last = u == len(parts) + 1
        acc = multiply(where, integrals, quads, groups, acc, begins[u - 2], parts[u - 2], TILE, cols, lanes, last)
        seen.append(acc)

    piece[0] = cut(0, 0, block)
    to_near(0)
    along(1)
    seen.append(first[0])
    to_far(0)
    along(2)
    seen.extend(gone[1])
    to_near(1)
    seen.append(both[0])
    swap(0)
    seen.append(first[1])
    to_far(1)
    seen.extend(gone[2])
    to_near(2)
    along(3)
    seen.append(both[1])
    swap(1)
    seen.append(first[2])
    to_far(2)
    seen.append(theirs[0])
    seen.append(theirs[1])
    seen.extend(gone[3])
    to_near(3)
    along(4)
    seen.append(both[2])
    swap(2)
    seen.append(first[3])
    to_far(3)
    seen.append(theirs[2])
    seen.extend(gone[4])
    to_near(4)
    seen.append(both[3])
    swap(3)
    seen.append(first[4])
    to_far(4)
    multiply_part(2)
    seen.append(theirs[3])
    seen.append(both[4])
    swap(4)
    multiply_part(3)
    seen.append(theirs[4])
    multiply_part(4)
    share = acc.shape[0] // cols
    mine = lambda c: lax.dynamic_slice(acc, (c * share, 0), (share, acc.shape[1]))
    got = [send(mine(col ^ d), "col", xor(cols, d)) for d in range(1, cols)]
    out = mine(col)
    for g in got:
        out = out + g
    return (0.5 * out[:, :height]).T


def plain(amplitudes, integrals):
    panel = lax.all_to_all(amplitudes, "col", split_axis=0, concat_axis=1, tiled=True)
    panel = lax.all_gather(panel, "row", axis=1, tiled=True)
    partial = jnp.dot(integrals, panel, preferred_element_type=F32, precision=lax.Precision.HIGH)
    return 0.5 * lax.psum_scatter(partial, "col", scatter_dimension=1, tiled=True)


def solution(mesh):
    rows, cols = mesh.shape["row"], mesh.shape["col"]

    def per_device(amplitudes, integrals):
        lanes, block = amplitudes.shape[1], integrals.shape[1]
        fits = rows == 8 and cols == 4 and lanes % SUB == 0 and block % (TILE * 8) == 0 and lanes * rows * cols % LANE == 0
        return (pipelined if fits else plain)(amplitudes, integrals)

    return jax.shard_map(
        per_device,
        mesh=mesh,
        in_specs=(P(None, ("row", "col")), P("row", "col")),
        out_specs=P("row", "col"),
        check_vma=False,
    )
```

time: 234 us -> 145 us (0.62)
  blocking collectives: 54.6 us -> 0 us
  matrix products: 51.3 us -> 0 us
  waiting for transfers between devices: 113 us -> 73.1 us
  starting transfers between devices: 0.04 us -> 32.1 us
  Pallas kernels: 0 us -> 31.6 us
  between operations: 13.4 us -> 0.27 us
  local copies, waits for them, and re-layouts: 0 us -> 2.83 us
    all_gather x1 -> x0, waiting for transfers between devices: 89.2 us -> none  [per_device(): lax.all_gather(cd_panel, 'row', axis=1, tiled=True)]
    ppermute x0 -> x25, waiting for transfers between devices: none -> 73.1 us  [send(): return lax.ppermute(lax.optimization_barrier((x, *seen))[0], axis, pairs)]
    all_to_all x1 -> x0, blocking collectives: 54.6 us -> none  [per_device(): lax.all_to_all(amplitudes, 'col', split_axis=0, concat_axis=1, tiled=True)]
    dot_general x1 -> x0, matrix products: 51.3 us -> none  [per_device(): jnp.dot(integrals, lax.all_gather(cd_panel, 'row', axis=1, tiled=True), p...]
    ppermute x0 -> x25, starting transfers between devices: none -> 32.1 us  [send(): return lax.ppermute(lax.optimization_barrier((x, *seen))[0], axis, pairs)]
    pallas_call x0 -> x3, Pallas kernels: none -> 31.6 us  [multiply(): pl.pallas_call(functools.partial(kernel, groups=groups, cols=cols, lanes=...]
    reduce_scatter x1 -> x0, waiting for transfers between devices: 23.4 us -> none  [per_device(): lax.psum_scatter(partial_value, 'col', scatter_dimension=1, tiled=True)]
    concatenate x0 -> x9, other arithmetic: none -> 2.65 us  [the longest x5 1.33 us: to_far(): pair = jnp.concatenate([piece[u], first[u]], 0)]
  transfers between devices with their start and end apart: 2 -> 25, of which waited for: 2 -> 14; matrix products, arithmetic and copies ran while one was open for 0% -> 2% of each run, Pallas kernels for 0% -> 16%
where the time goes in v1:
time: 145 us; the launch traced here: 143 us
  waiting for transfers between devices  73.1 us (50%)
  starting transfers between devices  32.1 us (22%)
  Pallas kernels  31.6 us (22%)
  other arithmetic  3.45 us (2%)
  local copies, waits for them, and re-layouts  2.83 us (2%)
    ppermute x25, waiting for transfers between devices, send(): return lax.ppermute(lax.optimization_barrier((x, *seen))[0], axis, pairs)  73.1 us
    ppermute x25, starting transfers between devices, send(): return lax.ppermute(lax.optimization_barrier((x, *seen))[0], axis, pairs)  32.1 us
    pallas_call x3, Pallas kernels, multiply(): pl.pallas_call(functools.partial(kernel, groups=groups, cols=cols, lanes=...  31.6 us
  transfers between devices with their start and end apart: 25, of which 14 were waited for; matrix products, arithmetic and copies ran while one was open for 2% of the time, Pallas kernels for 16%

profile of v1, /device:TPU:0, one launch (start us, length us, event | category | flops | bytes accessed | tf_op | source)
XLA Modules:
  0.0 143.5 jit_solution(5781232757273716588)
XLA Ops:
  0.0 2.2 %dynamic-slice_bitcast_fusion = (f32[8,16384]{1,0:T(8,128)}, f32[8,16384]{1,0:T(8,128)S(1)}) fusion(f32[65536,8]{0,1:T(8,128)} %param.2, s32[]{:T(128)S(6)} %select_n.50, s32[]{:T(128)S(6)} %select_n.49), kind=kLoop, calls=%fused_computation.6 | loop fusion | bytes 2097160 | tf_op jit(solution)/shard_map/dynamic_slice | solution.py:122
  2.2 2.9 %collective-permute-start = (f32[8,16384]{1,0:T(8,128)S(1)}, f32[8,16384]{1,0:T(8,128)}, u32[]{:S(2)}, u32[]{:S(2)}) collective-permute-start(f32[8,16384]{1,0:T(8,128)S(1)} %get-tuple-element.58), channel_id=1, source_target_pairs={{0,8},{4,20},{8,0},{12,28},{16,24},{20,4},{24,16},{28,12},{1,9},{5... | collective-permute-start | bytes 1572872 | tf_op jit(solution)/shard_map/ppermute | solution.py:119
  6.9 5.5 %collective-permute-done = f32[8,16384]{1,0:T(8,128)} collective-permute-done((f32[8,16384]{1,0:T(8,128)S(1)}, f32[8,16384]{1,0:T(8,128)}, u32[]{:S(2)}, u32[]{:S(2)}) %collective-permute-start) | collective-permute-done | bytes 524320 | tf_op jit(solution)/shard_map/ppermute | solution.py:119
  12.4 3.1 %collective-permute-start.6 = (f32[8,6144]{1,0:T(8,128)S(1)}, f32[8,6144]{1,0:T(8,128)S(1)}, u32[]{:S(2)}, u32[]{:S(2)}) collective-permute-start(f32[8,6144]{1,0:T(8,128)S(1)} %get-tuple-element.32), channel_id=1, source_target_pairs={{0,2},{1,3},{2,0},{3,1},{4,6},{5,7},{6,4},{7,5},{8,10},{9,11},{10,... | collective-permute-start | bytes 589832 | tf_op jit(solution)/shard_map/ppermute | solution.py:119
  18.0 1.6 %collective-permute-start.1 = (f32[16,16384]{1,0:T(8,128)S(1)}, f32[16,16384]{1,0:T(8,128)S(1)}, u32[]{:S(2)}, u32[]{:S(2)}) collective-permute-start(f32[16,16384]{1,0:T(8,128)S(1)} %pad_maximum_fusion.1), channel_id=1, source_target_pairs={{0,16},{4,12},{8,24},{12,4},{16,0},{20,28},{24,8},{28,20},{1,17},{... | collective-permute-start | bytes 3145736 | tf_op jit(solution)/shard_map/ppermute | solution.py:119
  19.6 3.2 %collective-permute-done.2 = f32[8,16384]{1,0:T(8,128)S(1)} collective-permute-done((f32[8,16384]{1,0:T(8,128)}, f32[8,16384]{1,0:T(8,128)S(1)}, u32[]{:S(2)}, u32[]{:S(2)}) %collective-permute-start.2) | collective-permute-done | bytes 524320 | tf_op jit(solution)/shard_map/ppermute | solution.py:119
  24.2 5.6 %collective-permute-done.6 = f32[8,6144]{1,0:T(8,128)S(1)} collective-permute-done((f32[8,6144]{1,0:T(8,128)S(1)}, f32[8,6144]{1,0:T(8,128)S(1)}, u32[]{:S(2)}, u32[]{:S(2)}) %collective-permute-start.6) | collective-permute-done | bytes 196640 | tf_op jit(solution)/shard_map/ppermute | solution.py:119
  29.9 6.1 %collective-permute-done.4 = f32[8,16384]{1,0:T(8,128)S(1)} collective-permute-done((f32[8,16384]{1,0:T(8,128)S(1)}, f32[8,16384]{1,0:T(8,128)S(1)}, u32[]{:S(2)}, u32[]{:S(2)}) %collective-permute-start.4) | collective-permute-done | bytes 524320 | tf_op jit(solution)/shard_map/ppermute | solution.py:119
  36.1 2.4 %collective-permute-done.1 = f32[16,16384]{1,0:T(8,128)S(1)} collective-permute-done((f32[16,16384]{1,0:T(8,128)S(1)}, f32[16,16384]{1,0:T(8,128)S(1)}, u32[]{:S(2)}, u32[]{:S(2)}) %collective-permute-start.1) | collective-permute-done | bytes 1048608 | tf_op jit(solution)/shard_map/ppermute | solution.py:119
  38.5 1.7 %collective-permute-start.10 = (f32[8,6144]{1,0:T(8,128)S(1)}, f32[8,6144]{1,0:T(8,128)S(1)}, u32[]{:S(2)}, u32[]{:S(2)}) collective-permute-start(f32[8,6144]{1,0:T(8,128)S(1)} %get-tuple-element.36), channel_id=1, source_target_pairs={{0,2},{1,3},{2,0},{3,1},{4,6},{5,7},{6,4},{7,5},{8,10},{9,11},{10,... | collective-permute-start | bytes 589832 | tf_op jit(solution)/shard_map/ppermute | solution.py:119
  45.4 6.3 %collective-permute-done.10 = f32[8,6144]{1,0:T(8,128)S(1)} collective-permute-done((f32[8,6144]{1,0:T(8,128)S(1)}, f32[8,6144]{1,0:T(8,128)S(1)}, u32[]{:S(2)}, u32[]{:S(2)}) %collective-permute-start.10) | collective-permute-done | bytes 196640 | tf_op jit(solution)/shard_map/ppermute | solution.py:119
  51.8 5.6 %collective-permute-done.5 = f32[16,16384]{1,0:T(8,128)S(1)} collective-permute-done((f32[16,16384]{1,0:T(8,128)S(1)}, f32[16,16384]{1,0:T(8,128)S(1)}, u32[]{:S(2)}, u32[]{:S(2)}) %collective-permute-start.5) | collective-permute-done | bytes 1048608 | tf_op jit(solution)/shard_map/ppermute | solution.py:119
  59.3 2.4 %collective-permute-done.8.refs_3_ = f32[32,16384]{1,0:T(8,128)S(1)} collective-permute-done((f32[32,16384]{1,0:T(8,128)S(1)}, f32[32,16384]{1,0:T(8,128)S(1)}, u32[]{:S(2)}, u32[]{:S(2)}) %collective-permute-start.8) | collective-permute-done | bytes 2097184 | tf_op jit(solution)/shard_map/ppermute | solution.py:119
  61.7 2.9 %collective-permute-start.13 = (f32[8,4096]{1,0:T(8,128)S(1)}, f32[8,4096]{1,0:T(8,128)S(1)}, u32[]{:S(2)}, u32[]{:S(2)}) collective-permute-start(f32[8,4096]{1,0:T(8,128)S(1)} %get-tuple-element.39), channel_id=1, source_target_pairs={{0,3},{1,2},{2,1},{3,0},{4,7},{5,6},{6,5},{7,4},{8,11},{9,10},{10,... | collective-permute-start | bytes 393224 | tf_op jit(solution)/shard_map/ppermute | solution.py:119
  64.6 5.2 %collective-permute-done.14 = f32[32,6144]{1,0:T(8,128)S(1)} collective-permute-done((f32[32,6144]{1,0:T(8,128)S(1)}, f32[32,6144]{1,0:T(8,128)S(1)}, u32[]{:S(2)}, u32[]{:S(2)}) %collective-permute-start.14) | collective-permute-done | bytes 786464 | tf_op jit(solution)/shard_map/ppermute | solution.py:119
  71.4 4.6 %collective-permute-done.12 = f32[8,4096]{1,0:T(8,128)S(1)} collective-permute-done((f32[8,4096]{1,0:T(8,128)S(1)}, f32[8,4096]{1,0:T(8,128)S(1)}, u32[]{:S(2)}, u32[]{:S(2)}) %collective-permute-start.12) | collective-permute-done | bytes 131104 | tf_op jit(solution)/shard_map/ppermute | solution.py:119
  76.0 1.7 %collective-permute-done.15 = f32[16,6144]{1,0:T(8,128)S(1)} collective-permute-done((f32[16,6144]{1,0:T(8,128)S(1)}, f32[16,6144]{1,0:T(8,128)S(1)}, u32[]{:S(2)}, u32[]{:S(2)}) %collective-permute-start.15) | collective-permute-done | bytes 393248 | tf_op jit(solution)/shard_map/ppermute | solution.py:119
  80.4 10.9 %collective-permute-done.18 = f32[32,6144]{1,0:T(8,128)S(1)} collective-permute-done((f32[32,6144]{1,0:T(8,128)S(1)}, f32[32,6144]{1,0:T(8,128)S(1)}, u32[]{:S(2)}, u32[]{:S(2)}) %collective-permute-start.18) | collective-permute-done | bytes 786464 | tf_op jit(solution)/shard_map/ppermute | solution.py:119
  92.5 11.4 %shard_map.28 = f32[704,256]{1,0:T(8,128)S(1)} custom-call(s32[3]{0:T(128)S(1)} %pad_add_fusion.where, f32[704,16384]{1,0:T(8,128)} %v_ref.5, f32[32,16384]{1,0:T(8,128)S(1)} %pad_maximum_fusion.refs_0_, f32[32,16384]{1,0:T(8,128)S(1)} %collective-permute-done.3.refs_1_, f32[32,16384]{1,0:T(8,128)S(1)} %constant_dynamic-update-slice_fusion.refs_2_, ...), custom_call_target="tpu_custom_call" | custom-call | flops 19931332608 | bytes 70778880 | tf_op jit(solution)/shard_map/pallas_call | solution.py:86
  104.2 11.4 %shard_map.29.refs_6_ = f32[704,256]{1,0:T(8,128)S(1)} custom-call(s32[3]{0:T(128)S(1)} %pad_add_fusion.where, f32[704,16384]{1,0:T(8,128)} %v_ref.5, f32[32,16384]{1,0:T(8,128)S(1)} %pad_maximum_fusion.refs_0_, f32[32,16384]{1,0:T(8,128)S(1)} %collective-permute-done.3.refs_1_, ...), custom_call_target="tpu_custom_call", output_to_operand_aliasing={{}: (8, {})} | custom-call | flops 19931332608 | bytes 70778880 | tf_op jit(solution)/shard_map/pallas_call | solution.py:86
  115.7 8.9 %shard_map.30 = f32[256,768]{1,0:T(8,128)S(1)} custom-call(s32[3]{0:T(128)S(1)} %pad_add_fusion.where, f32[704,16384]{1,0:T(8,128)} %v_ref.5, f32[32,16384]{1,0:T(8,128)S(1)} %pad_maximum_fusion.refs_0_, f32[32,16384]{1,0:T(8,128)S(1)} %collective-permute-done.3.refs_1_, f32[32,16384]{1,0:T(8,128)S(1)} %constant_dynamic-update-slice_fusion.refs_2_, ...), custom_call_target="tpu_custom_call" | custom-call | flops 13287555072 | bytes 47185920 | tf_op jit(solution)/shard_map/pallas_call | solution.py:86
  125.6 2.5 %collective-permute-start.23 = (f32[64,768]{1,0:T(8,128)S(1)}, f32[64,768]{1,0:T(8,128)S(1)}, u32[]{:S(2)}, u32[]{:S(2)}) collective-permute-start(f32[64,768]{1,0:T(8,128)S(1)} %get-tuple-element.49), channel_id=1, source_target_pairs={{0,2},{1,3},{2,0},{3,1},{4,6},{5,7},{6,4},{7,5},{8,10},{9,11},{10,... | collective-permute-start | bytes 589832 | tf_op jit(solution)/shard_map/ppermute | solution.py:119
  129.1 6.5 %collective-permute-done.22 = f32[64,768]{1,0:T(8,128)S(1)} collective-permute-done((f32[64,768]{1,0:T(8,128)S(1)}, f32[64,768]{1,0:T(8,128)S(1)}, u32[]{:S(2)}, u32[]{:S(2)}) %collective-permute-start.22) | collective-permute-done | bytes 196640 | tf_op jit(solution)/shard_map/ppermute | solution.py:119
  135.5 7.2 %collective-permute-done.23 = f32[64,768]{1,0:T(8,128)S(1)} collective-permute-done((f32[64,768]{1,0:T(8,128)S(1)}, f32[64,768]{1,0:T(8,128)S(1)}, u32[]{:S(2)}, u32[]{:S(2)}) %collective-permute-start.23) | collective-permute-done | bytes 196640 | tf_op jit(solution)/shard_map/ppermute | solution.py:119
  (62 shorter events, 21.4 us)
Async XLA Ops:
  2.2 10.2 %collective-permute-start = (f32[8,16384]{1,0:T(8,128)S(1)}, f32[8,16384]{1,0:T(8,128)}, u32[]{:S(2)}, u32[]{:S(2)}) collective-permute-start(f32[8,16384]{1,0:T(8,128)S(1)} %get-tuple-element.58), channel_id=1, source_target_pairs={{0,8},{4,20},{8,0},{12,28},{16,24},{20,4},{24,16},{28,12},{1,9},{5... | collective-permute-start | bytes 1572872 | tf_op jit(solution)/shard_map/ppermute | solution.py:119
  5.2 17.6 %collective-permute-start.2 = (f32[8,16384]{1,0:T(8,128)}, f32[8,16384]{1,0:T(8,128)S(1)}, u32[]{:S(2)}, u32[]{:S(2)}) collective-permute-start(f32[8,16384]{1,0:T(8,128)} %get-tuple-element.57), channel_id=1, source_target_pairs={{0,1},{1,0},{2,3},{3,2},{4,5},{5,4},{6,7},{7,6},{8,9},{9,8},{10,11... | collective-permute-start | bytes 1572872 | tf_op jit(solution)/shard_map/ppermute | solution.py:119
  12.4 17.4 %collective-permute-start.6 = (f32[8,6144]{1,0:T(8,128)S(1)}, f32[8,6144]{1,0:T(8,128)S(1)}, u32[]{:S(2)}, u32[]{:S(2)}) collective-permute-start(f32[8,6144]{1,0:T(8,128)S(1)} %get-tuple-element.32), channel_id=1, source_target_pairs={{0,2},{1,3},{2,0},{3,1},{4,6},{5,7},{6,4},{7,5},{8,10},{9,11},{10,... | collective-permute-start | bytes 589832 | tf_op jit(solution)/shard_map/ppermute | solution.py:119
  15.6 14.3 %collective-permute-start.7 = (f32[8,6144]{1,0:T(8,128)S(1)}, f32[8,6144]{1,0:T(8,128)S(1)}, u32[]{:S(2)}, u32[]{:S(2)}) collective-permute-start(f32[8,6144]{1,0:T(8,128)S(1)} %get-tuple-element.33), channel_id=1, source_target_pairs={{0,3},{1,2},{2,1},{3,0},{4,7},{5,6},{6,5},{7,4},{8,11},{9,10},{10,... | collective-permute-start | bytes 589832 | tf_op jit(solution)/shard_map/ppermute | solution.py:119
  18.0 20.5 %collective-permute-start.1 = (f32[16,16384]{1,0:T(8,128)S(1)}, f32[16,16384]{1,0:T(8,128)S(1)}, u32[]{:S(2)}, u32[]{:S(2)}) collective-permute-start(f32[16,16384]{1,0:T(8,128)S(1)} %pad_maximum_fusion.1), channel_id=1, source_target_pairs={{0,16},{4,12},{8,24},{12,4},{16,0},{20,28},{24,8},{28,20},{1,17},{... | collective-permute-start | bytes 3145736 | tf_op jit(solution)/shard_map/ppermute | solution.py:119
  22.8 13.2 %collective-permute-start.4 = (f32[8,16384]{1,0:T(8,128)S(1)}, f32[8,16384]{1,0:T(8,128)S(1)}, u32[]{:S(2)}, u32[]{:S(2)}) collective-permute-start(f32[8,16384]{1,0:T(8,128)S(1)} %collective-permute-done.2), channel_id=1, source_target_pairs={{0,8},{4,20},{8,0},{12,28},{16,24},{20,4},{24,16},{28,12},{1,9},{5... | collective-permute-start | bytes 1572872 | tf_op jit(solution)/shard_map/ppermute | solution.py:119
  38.5 13.2 %collective-permute-start.10 = (f32[8,6144]{1,0:T(8,128)S(1)}, f32[8,6144]{1,0:T(8,128)S(1)}, u32[]{:S(2)}, u32[]{:S(2)}) collective-permute-start(f32[8,6144]{1,0:T(8,128)S(1)} %get-tuple-element.36), channel_id=1, source_target_pairs={{0,2},{1,3},{2,0},{3,1},{4,6},{5,7},{6,4},{7,5},{8,10},{9,11},{10,... | collective-permute-start | bytes 589832 | tf_op jit(solution)/shard_map/ppermute | solution.py:119
  40.2 11.5 %collective-permute-start.11 = (f32[8,6144]{1,0:T(8,128)S(1)}, f32[8,6144]{1,0:T(8,128)S(1)}, u32[]{:S(2)}, u32[]{:S(2)}) collective-permute-start(f32[8,6144]{1,0:T(8,128)S(1)} %get-tuple-element.37), channel_id=1, source_target_pairs={{0,3},{1,2},{2,1},{3,0},{4,7},{5,6},{6,5},{7,4},{8,11},{9,10},{10,... | collective-permute-start | bytes 589832 | tf_op jit(solution)/shard_map/ppermute | solution.py:119
  41.1 16.6 %collective-permute-start.9 = (f32[16,6144]{1,0:T(8,128)S(1)}, f32[16,6144]{1,0:T(8,128)S(1)}, u32[]{:S(2)}, u32[]{:S(2)}) collective-permute-start(f32[16,6144]{1,0:T(8,128)S(1)} %pad_maximum_fusion.6), channel_id=1, source_target_pairs={{0,8},{4,20},{8,0},{12,28},{16,24},{20,4},{24,16},{28,12},{1,9},{5... | collective-permute-start | bytes 1179656 | tf_op jit(solution)/shard_map/ppermute | solution.py:119
  42.6 14.8 %collective-permute-start.5 = (f32[16,16384]{1,0:T(8,128)S(1)}, f32[16,16384]{1,0:T(8,128)S(1)}, u32[]{:S(2)}, u32[]{:S(2)}) collective-permute-start(f32[16,16384]{1,0:T(8,128)S(1)} %pad_maximum_fusion.2), channel_id=1, source_target_pairs={{0,16},{4,12},{8,24},{12,4},{16,0},{20,28},{24,8},{28,20},{1,17},{... | collective-permute-start | bytes 3145736 | tf_op jit(solution)/shard_map/ppermute | solution.py:119
  45.3 13.9 %collective-permute-start.3 = (f32[32,16384]{1,0:T(8,128)S(1)}, f32[32,16384]{1,0:T(8,128)S(1)}, u32[]{:S(2)}, u32[]{:S(2)}) collective-permute-start(f32[32,16384]{1,0:T(8,128)S(1)} %pad_maximum_fusion.refs_0_), channel_id=1, source_target_pairs={{0,4},{4,0},{8,12},{12,8},{16,20},{20,16},{24,28},{28,24},{1,5},{5... | collective-permute-start | bytes 6291464 | tf_op jit(solution)/shard_map/ppermute | solution.py:119
  57.7 12.1 %collective-permute-start.14 = (f32[32,6144]{1,0:T(8,128)S(1)}, f32[32,6144]{1,0:T(8,128)S(1)}, u32[]{:S(2)}, u32[]{:S(2)}) collective-permute-start(f32[32,6144]{1,0:T(8,128)S(1)} %pad_maximum_fusion.3), channel_id=1, source_target_pairs={{0,16},{4,12},{8,24},{12,4},{16,0},{20,28},{24,8},{28,20},{1,17},{... | collective-permute-start | bytes 2359304 | tf_op jit(solution)/shard_map/ppermute | solution.py:119
  61.7 9.7 %collective-permute-start.13 = (f32[8,4096]{1,0:T(8,128)S(1)}, f32[8,4096]{1,0:T(8,128)S(1)}, u32[]{:S(2)}, u32[]{:S(2)}) collective-permute-start(f32[8,4096]{1,0:T(8,128)S(1)} %get-tuple-element.39), channel_id=1, source_target_pairs={{0,3},{1,2},{2,1},{3,0},{4,7},{5,6},{6,5},{7,4},{8,11},{9,10},{10,... | collective-permute-start | bytes 393224 | tf_op jit(solution)/shard_map/ppermute | solution.py:119
  64.6 11.4 %collective-permute-start.12 = (f32[8,4096]{1,0:T(8,128)S(1)}, f32[8,4096]{1,0:T(8,128)S(1)}, u32[]{:S(2)}, u32[]{:S(2)}) collective-permute-start(f32[8,4096]{1,0:T(8,128)S(1)} %get-tuple-element.38), channel_id=1, source_target_pairs={{0,2},{1,3},{2,0},{3,1},{4,6},{5,7},{6,4},{7,5},{8,10},{9,11},{10,... | collective-permute-start | bytes 393224 | tf_op jit(solution)/shard_map/ppermute | solution.py:119
  69.8 7.8 %collective-permute-start.15 = (f32[16,6144]{1,0:T(8,128)S(1)}, f32[16,6144]{1,0:T(8,128)S(1)}, u32[]{:S(2)}, u32[]{:S(2)}) collective-permute-start(f32[16,6144]{1,0:T(8,128)S(1)} %pad_maximum_fusion.7), channel_id=1, source_target_pairs={{0,8},{4,20},{8,0},{12,28},{16,24},{20,4},{24,16},{28,12},{1,9},{5... | collective-permute-start | bytes 1179656 | tf_op jit(solution)/shard_map/ppermute | solution.py:119
  71.4 7.9 %collective-permute-start.16 = (f32[64,6144]{1,0:T(8,128)S(1)}, f32[64,6144]{1,0:T(8,128)S(1)}, u32[]{:S(2)}, u32[]{:S(2)}) collective-permute-start(f32[64,6144]{1,0:T(8,128)S(1)} %constant_dynamic-update-slice_fusion.3.refs_4_), channel_id=1, source_target_pairs={{0,4},{4,0},{8,12},{12,8},{16,20},{20,16},{24,28},{28,24},{1,5},{5... | collective-permute-start | bytes 4718600 | tf_op jit(solution)/shard_map/ppermute | solution.py:119
  77.7 13.5 %collective-permute-start.18 = (f32[32,6144]{1,0:T(8,128)S(1)}, f32[32,6144]{1,0:T(8,128)S(1)}, u32[]{:S(2)}, u32[]{:S(2)}) collective-permute-start(f32[32,6144]{1,0:T(8,128)S(1)} %pad_maximum_fusion.4), channel_id=1, source_target_pairs={{0,16},{4,12},{8,24},{12,4},{16,0},{20,28},{24,8},{28,20},{1,17},{... | collective-permute-start | bytes 2359304 | tf_op jit(solution)/shard_map/ppermute | solution.py:119
  79.3 12.1 %collective-permute-start.17 = (f32[16,4096]{1,0:T(8,128)S(1)}, f32[16,4096]{1,0:T(8,128)S(1)}, u32[]{:S(2)}, u32[]{:S(2)}) collective-permute-start(f32[16,4096]{1,0:T(8,128)S(1)} %pad_maximum_fusion.8), channel_id=1, source_target_pairs={{0,8},{4,20},{8,0},{12,28},{16,24},{20,4},{24,16},{28,12},{1,9},{5... | collective-permute-start | bytes 786440 | tf_op jit(solution)/shard_map/ppermute | solution.py:119
  91.3 12.7 %collective-permute-start.20 = (f32[64,6144]{1,0:T(8,128)S(1)}, f32[64,6144]{1,0:T(8,128)S(1)}, u32[]{:S(2)}, u32[]{:S(2)}) collective-permute-start(f32[64,6144]{1,0:T(8,128)S(1)} %constant_dynamic-update-slice_fusion.11.refs_4_), channel_id=1, source_target_pairs={{0,4},{4,0},{8,12},{12,8},{16,20},{20,16},{24,28},{28,24},{1,5},{5... | collective-permute-start | bytes 4718600 | tf_op jit(solution)/shard_map/ppermute | solution.py:119
  91.5 12.5 %collective-permute-start.19 = (f32[32,4096]{1,0:T(8,128)S(1)}, f32[32,4096]{1,0:T(8,128)S(1)}, u32[]{:S(2)}, u32[]{:S(2)}) collective-permute-start(f32[32,4096]{1,0:T(8,128)S(1)} %pad_maximum_fusion.5), channel_id=1, source_target_pairs={{0,16},{4,12},{8,24},{12,4},{16,0},{20,28},{24,8},{28,20},{1,17},{... | collective-permute-start | bytes 1572872 | tf_op jit(solution)/shard_map/ppermute | solution.py:119
  104.0 11.7 %collective-permute-start.21 = (f32[64,4096]{1,0:T(8,128)S(1)}, f32[64,4096]{1,0:T(8,128)S(1)}, u32[]{:S(2)}, u32[]{:S(2)}) collective-permute-start(f32[64,4096]{1,0:T(8,128)S(1)} %constant_dynamic-update-slice_fusion.7.refs_4_), channel_id=1, source_target_pairs={{0,4},{4,0},{8,12},{12,8},{16,20},{20,16},{24,28},{28,24},{1,5},{5... | collective-permute-start | bytes 3145736 | tf_op jit(solution)/shard_map/ppermute | solution.py:119
  124.6 10.9 %collective-permute-start.22 = (f32[64,768]{1,0:T(8,128)S(1)}, f32[64,768]{1,0:T(8,128)S(1)}, u32[]{:S(2)}, u32[]{:S(2)}) collective-permute-start(f32[64,768]{1,0:T(8,128)S(1)} %get-tuple-element.48), channel_id=1, source_target_pairs={{0,1},{1,0},{2,3},{3,2},{4,5},{5,4},{6,7},{7,6},{8,9},{9,8},{10,11... | collective-permute-start | bytes 589832 | tf_op jit(solution)/shard_map/ppermute | solution.py:119
  125.6 17.1 %collective-permute-start.23 = (f32[64,768]{1,0:T(8,128)S(1)}, f32[64,768]{1,0:T(8,128)S(1)}, u32[]{:S(2)}, u32[]{:S(2)}) collective-permute-start(f32[64,768]{1,0:T(8,128)S(1)} %get-tuple-element.49), channel_id=1, source_target_pairs={{0,2},{1,3},{2,0},{3,1},{4,6},{5,7},{6,4},{7,5},{8,10},{9,11},{10,... | collective-permute-start | bytes 589832 | tf_op jit(solution)/shard_map/ppermute | solution.py:119
  128.2 14.6 %collective-permute-start.24 = (f32[64,768]{1,0:T(8,128)S(1)}, f32[64,768]{1,0:T(8,128)S(1)}, u32[]{:S(2)}, u32[]{:S(2)}) collective-permute-start(f32[64,768]{1,0:T(8,128)S(1)} %get-tuple-element.50), channel_id=1, source_target_pairs={{0,3},{1,2},{2,1},{3,0},{4,7},{5,6},{6,5},{7,4},{8,11},{9,10},{10,... | collective-permute-start | bytes 589832 | tf_op jit(solution)/shard_map/ppermute | solution.py:119
  (2 other events, 11.0 us)

commit v2 on v1

v2 whole, which is shorter than its diff:
```python
import functools

import jax
import jax.numpy as jnp
from jax import lax
from jax.experimental import pallas as pl
from jax.experimental.pallas import tpu as pltpu
from jax.sharding import PartitionSpec as P

F32, BF16 = jnp.float32, jnp.bfloat16
NT = (((1,), (1,)), ((), ()))
SUB, LANE, MXU = 8, 128, 256

PARTS = (3, 3, 2)
TILE, LIMIT = 2048, 28
COST = 3


def split(x):
    hi = x.astype(BF16)
    return hi, (x - hi.astype(F32)).astype(BF16)


def product(v, t):
    dot = lambda a, b: lax.dot_general(a, b, NT, preferred_element_type=F32)
    vh, vl = split(v)
    th, tl = split(t)
    n = t.shape[0]
    if 2 * n <= MXU:
        wide = dot(vh, jnp.concatenate([th, tl], 0))
        return wide[:, :n] + (wide[:, n:] + dot(vl, th))
    return dot(vh, th) + (dot(vh, tl) + dot(vl, th))


def kernel(where, v_ref, *refs, groups, lanes, acc, last):
    step = pl.program_id(0)
    if last:
        out_ref, tau, total = refs[-3:]
    else:
        out_ref, tau = refs[-2:]
        total = out_ref
    chip, core = where[0], where[1]
    for g, (half, begin, planes) in enumerate(groups):
        for other in range(2):
            its = core if other == 0 else 1 - core
            one, two = its + 1, 2 - its
            for m, source in enumerate((chip, chip ^ one, chip ^ two, chip ^ 3)):
                at = half * 16 * lanes + ((source * 2 + its) * 2 + begin) * lanes
                size = planes * lanes
                ref = refs[4 * g + 2 * other + m // 2]
                tau[pl.ds(pl.multiple_of(at, lanes), size), :] = ref[pl.ds(m % 2 * size, size), :]
    new = product(v_ref[...], tau[...])

    @pl.when(step == 0)
    def _():
        total[...] = new + refs[4 * len(groups)][...] if acc else new

    @pl.when(step > 0)
    def _():
        total[...] += new

    if last:

        @pl.when(step == pl.num_programs(0) - 1)
        def _():
            rows = total.shape[0]
            out_ref[:, :rows] = total[...].T
            if rows < out_ref.shape[1]:
                out_ref[:, rows:] = jnp.zeros((out_ref.shape[0], out_ref.shape[1] - rows), F32)


def multiply(where, v, quads, acc, at, width, tile, lanes, last):
    rows = v.shape[0]
    groups = tuple(q[0] for q in quads)
    ij = len({g[0] for g in groups}) * 16 * lanes
    lowest = min(g[0] for g in groups)
    groups = tuple((half - lowest, begin, planes) for half, begin, planes in groups)
    specs, operands = [pl.BlockSpec((rows, tile), lambda i, w: (0, i + at // tile))], [v]
    for _, pieces, begin in quads:
        for a in pieces:
            specs.append(pl.BlockSpec((a.shape[0], tile), lambda i, w, b=begin: (0, i + (at - b) // tile)))
            operands.append(a)
    if acc is not None:
        specs.append(pl.BlockSpec((rows, ij), lambda i, w: (0, acc[1])))
        operands.append(acc[0])
    scratch = [pltpu.VMEM((ij, tile), F32)]
    if last:
        shape = (ij, pl.cdiv(rows, LANE) * LANE)
        spec = pl.BlockSpec(shape, lambda i, w: (0, 0))
        scratch.append(pltpu.VMEM((rows, ij), F32))
    else:
        shape, spec = (rows, ij), pl.BlockSpec((rows, ij), lambda i, w: (0, 0))
    return pl.pallas_call(
        functools.partial(kernel, groups=groups, lanes=lanes, acc=acc is not None, last=last),
        grid_spec=pltpu.PrefetchScalarGridSpec(
            num_scalar_prefetch=1, grid=(width // tile,), in_specs=specs, out_specs=spec, scratch_shapes=scratch
        ),
        out_shape=jax.ShapeDtypeStruct(shape, F32),
        cost_estimate=pl.CostEstimate(
            flops=COST * 6 * rows * ij * width, bytes_accessed=COST * 4 * (rows + ij) * width, transcendentals=0
        ),
        compiler_params=pltpu.CompilerParams(vmem_limit_bytes=LIMIT << 20),
    )(where, *operands)


def xor(n, bits):
    return [(i, i ^ bits) for i in range(n)]


def pipelined(amplitudes, integrals):
    tau = amplitudes.T
    lanes, (height, block) = tau.shape[0], integrals.shape
    row, col = lax.axis_index("row"), lax.axis_index("col")
    rows, cols = lax.axis_size("row"), lax.axis_size("col")
    where = jnp.stack([row // 2, row % 2]).astype(jnp.int32)
    near = [(i, i ^ (2 if i % 2 == 0 else 4)) for i in range(rows)]
    far = [(i, i ^ (4 if i % 2 == 0 else 2)) for i in range(rows)]
    parts = [p * block // 8 for p in PARTS]
    begins = [sum(parts[:i]) for i in range(len(parts) + 1)]
    seen = []
    piece, first, pair, both, their_pair, their_both, gone = {}, {}, {}, {}, {}, {}, {}
    totals, sums = [None, None], [None, None]

    def send(x, axis, pairs):
        return lax.ppermute(lax.optimization_barrier((x, *seen))[0], axis, pairs)

    def cut(d, begin, width):
        return lax.dynamic_slice(tau, (0, (col ^ d) * block + begin), (lanes, width))

    def along(u):
        if u == 1:
            gone[u] = [send(cut(1, 0, block), "col", xor(cols, 1))]
        else:
            gone[u] = [send(cut(d, begins[u - 2], parts[u - 2]), "col", xor(cols, d)) for d in range(2, cols)]
        piece[u] = jnp.concatenate(gone[u], 0)

    def to_near(u):
        first[u] = send(piece[u], "row", near)
        pair[u] = jnp.concatenate([piece[u], first[u]], 0)

    def to_far(u):
        both[u] = send(pair[u], "row", far)

    def swap_pair(u):
        their_pair[u] = send(pair[u], "row", xor(rows, 1))

    def swap_both(u):
        their_both[u] = send(both[u], "row", xor(rows, 1))

    def have(u):
        return pair[u], both[u], their_pair[u], their_both[u]

    def times(halves, begin, width):
        quads = []
        if 0 in halves:
            quads += [((0, u, 1), have(u), 0) for u in (0, 1)]
        if 1 in halves:
            u = begins.index(begin) + 2
            quads.append(((1, 0, 2), have(u), begin))
        last = begin + width == block
        acc = multiply(where, integrals, quads, totals[halves[0]], begin, width, TILE, lanes, last)
        for place, half in enumerate(halves):
            totals[half] = (acc, place)
        seen.append(acc)

    def add_up(half):
        acc, place = totals[half]
        share = 4 * lanes
        mine = lambda c: lax.dynamic_slice(acc, ((place * cols + c) * share, 0), (share, acc.shape[1]))
        sums[half] = [mine(col)] + [send(mine(col ^ d), "col", xor(cols, d)) for d in range(1, cols)]

    piece[0] = cut(0, 0, block)
    to_near(0)
    along(1)
    seen.append(first[0])
    to_far(0)
    swap_pair(0)
    along(2)
    seen.extend(gone[1])
    to_near(1)
    seen.append(both[0])
    swap_both(0)
    seen.append(first[1])
    to_far(1)
    swap_pair(1)
    seen.extend(gone[2])
    to_near(2)
    along(3)
    seen.append(both[1])
    swap_both(1)
    seen.append(first[2])
    to_far(2)
    swap_pair(2)
    seen.append(their_pair[0])
    seen.append(their_both[0])
    seen.append(their_pair[1])
    seen.append(their_both[1])
    seen.extend(gone[3])
    to_near(3)
    along(4)
    seen.append(both[2])
    swap_both(2)
    seen.append(first[3])
    to_far(3)
    swap_pair(3)
    seen.append(their_pair[2])
    seen.append(their_both[2])
    seen.extend(gone[4])
    to_near(4)
    times((0, 1), begins[0], parts[0])
    seen.append(first[4])
    to_far(4)
    swap_pair(4)
    seen.append(both[3])
    swap_both(3)
    seen.append(their_pair[3])
    seen.append(their_both[3])
    times((0, 1), begins[1], parts[1])
    seen.append(both[4])
    swap_both(4)
    seen.append(their_pair[4])
    seen.append(their_both[4])
    times((0,), begins[2], parts[2])
    add_up(0)
    times((1,), begins[2], parts[2])
    add_up(1)
    planes = [[] for _ in range(cols)]
    for half in range(2):
        for s in range(cols):
            x = sums[half][s].reshape(2, 2, lanes, -1)
            for k in range(2):
                planes[s ^ (2 * half + k)].append(x[:, k])
    out = [0.5 * functools.reduce(jnp.add, p) for p in planes]
    low, high = (col & 1) == 1, (col & 2) == 2
    out = [jnp.where(low, out[d ^ 1], out[d]) for d in range(cols)]
    out = [jnp.where(high, out[d ^ 2], out[d]) for d in range(cols)]
    return jnp.stack(out, 1).reshape(2 * cols * lanes, -1)[:, :height].T


def plain(amplitudes, integrals):
    panel = lax.all_to_all(amplitudes, "col", split_axis=0, concat_axis=1, tiled=True)
    panel = lax.all_gather(panel, "row", axis=1, tiled=True)
    partial = jnp.dot(integrals, panel, preferred_element_type=F32, precision=lax.Precision.HIGH)
    return 0.5 * lax.psum_scatter(partial, "col", scatter_dimension=1, tiled=True)


def solution(mesh):
    rows, cols = mesh.shape["row"], mesh.shape["col"]

    def per_device(amplitudes, integrals):
        lanes, block = amplitudes.shape[1], integrals.shape[1]
        fits = rows == 8 and cols == 4 and lanes % SUB == 0 and block % (TILE * 8) == 0 and lanes * rows * cols % LANE == 0
        return (pipelined if fits else plain)(amplitudes, integrals)

    return jax.shard_map(
        per_device,
        mesh=mesh,
        in_specs=(P(None, ("row", "col")), P("row", "col")),
        out_specs=P("row", "col"),
        check_vma=False,
    )
```

time: 145 us -> 136 us (0.938); the launches traced: 143 us -> 136 us
  waiting for transfers between devices: 73.1 us -> 55.5 us
  starting transfers between devices: 32.1 us -> 38.9 us
  Pallas kernels: 31.6 us -> 37 us
  other arithmetic: 3.45 us -> 1.34 us
    ppermute x25 -> x33, waiting for transfers between devices: 73.1 us -> 55.5 us  [send(): return lax.ppermute(lax.optimization_barrier((x, *seen))[0], axis, pairs)]
    ppermute x25 -> x33, starting transfers between devices: 32.1 us -> 38.9 us  [send(): return lax.ppermute(lax.optimization_barrier((x, *seen))[0], axis, pairs)]
    pallas_call x3 -> x4, Pallas kernels: 31.6 us -> 37 us  [multiply(): pl.pallas_call(functools.partial(kernel, groups=groups, lanes=lanes, acc=...]
    concatenate x6 -> x1, other arithmetic: 2.58 us -> 1.11 us  [to_near(): pair[u] = jnp.concatenate([piece[u], first[u]], 0)]
  transfers between devices with their start and end apart: 25 -> 33, of which waited for: 14 -> 11; matrix products, arithmetic and copies ran while one was open for 2% -> 1% of each run, Pallas kernels for 16% -> 27%
where the time goes in v2:
time: 136 us
  waiting for transfers between devices  55.5 us (41%)
  starting transfers between devices  38.9 us (29%)
  Pallas kernels  37 us (27%)
  local copies, waits for them, and re-layouts  3.29 us (2%)
    ppermute x33, waiting for transfers between devices, send(): return lax.ppermute(lax.optimization_barrier((x, *seen))[0], axis, pairs)  55.5 us
    ppermute x33, starting transfers between devices, send(): return lax.ppermute(lax.optimization_barrier((x, *seen))[0], axis, pairs)  38.9 us
    pallas_call x4, Pallas kernels, multiply(): pl.pallas_call(functools.partial(kernel, groups=groups, lanes=lanes, acc=...  37 us
  transfers between devices with their start and end apart: 33, of which 11 were waited for; matrix products, arithmetic and copies ran while one was open for 1% of the time, Pallas kernels for 27%

profile of v2, /device:TPU:0, one launch (start us, length us, event | category | flops | bytes accessed | tf_op | source)
XLA Modules:
  0.0 136.3 jit_solution(3092893707241050672)
XLA Ops:
  0.0 2.2 %dynamic-slice_bitcast_fusion = (f32[8,16384]{1,0:T(8,128)}, f32[8,16384]{1,0:T(8,128)S(1)}) fusion(f32[65536,8]{0,1:T(8,128)} %param.2, s32[]{:T(128)S(6)} %select_n.106, s32[]{:T(128)S(6)} %select_n.105), kind=kLoop, calls=%fused_computation.1 | loop fusion | bytes 2097160 | tf_op jit(solution)/shard_map/dynamic_slice | solution.py:128
  2.2 2.9 %collective-permute-start = (f32[8,16384]{1,0:T(8,128)S(1)}, f32[8,16384]{1,0:T(8,128)}, u32[]{:S(2)}, u32[]{:S(2)}) collective-permute-start(f32[8,16384]{1,0:T(8,128)S(1)} %get-tuple-element.69), channel_id=1, source_target_pairs={{0,8},{4,20},{8,0},{12,28},{16,24},{20,4},{24,16},{28,12},{1,9},{5... | collective-permute-start | bytes 1572872 | tf_op jit(solution)/shard_map/ppermute | solution.py:125
  5.2 1.6 %collective-permute-start.3 = (f32[8,16384]{1,0:T(8,128)}, f32[8,16384]{1,0:T(8,128)S(1)}, u32[]{:S(2)}, u32[]{:S(2)}) collective-permute-start(f32[8,16384]{1,0:T(8,128)} %get-tuple-element.68), channel_id=1, source_target_pairs={{0,1},{1,0},{2,3},{3,2},{4,5},{5,4},{6,7},{7,6},{8,9},{9,8},{10,11... | collective-permute-start | bytes 1572872 | tf_op jit(solution)/shard_map/ppermute | solution.py:125
  6.9 5.5 %collective-permute-done = f32[8,16384]{1,0:T(8,128)} collective-permute-done((f32[8,16384]{1,0:T(8,128)S(1)}, f32[8,16384]{1,0:T(8,128)}, u32[]{:S(2)}, u32[]{:S(2)}) %collective-permute-start) | collective-permute-done | bytes 524320 | tf_op jit(solution)/shard_map/ppermute | solution.py:125
  13.5 2.1 %collective-permute-start.1 = (f32[16,16384]{1,0:T(8,128)S(1)}, f32[16,16384]{1,0:T(8,128)S(1)}, u32[]{:S(2)}, u32[]{:S(2)}) collective-permute-start(f32[16,16384]{1,0:T(8,128)S(1)} %pad_maximum_fusion.refs_0_), channel_id=1, source_target_pairs={{0,16},{4,12},{8,24},{12,4},{16,0},{20,28},{24,8},{28,20},{1,17},{... | collective-permute-start | bytes 3145736 | tf_op jit(solution)/shard_map/ppermute | solution.py:125
  15.7 2.6 %collective-permute-start.8 = (f32[8,6144]{1,0:T(8,128)S(1)}, f32[8,6144]{1,0:T(8,128)S(1)}, u32[]{:S(2)}, u32[]{:S(2)}) collective-permute-start(f32[8,6144]{1,0:T(8,128)S(1)} %get-tuple-element.35), channel_id=1, source_target_pairs={{0,2},{1,3},{2,0},{3,1},{4,6},{5,7},{6,4},{7,5},{8,10},{9,11},{10,... | collective-permute-start | bytes 589832 | tf_op jit(solution)/shard_map/ppermute | solution.py:125
  19.6 1.5 %collective-permute-start.5 = (f32[8,16384]{1,0:T(8,128)S(1)}, f32[8,16384]{1,0:T(8,128)S(1)}, u32[]{:S(2)}, u32[]{:S(2)}) collective-permute-start(f32[8,16384]{1,0:T(8,128)S(1)} %collective-permute-done.3), channel_id=1, source_target_pairs={{0,8},{4,20},{8,0},{12,28},{16,24},{20,4},{24,16},{28,12},{1,9},{5... | collective-permute-start | bytes 1572872 | tf_op jit(solution)/shard_map/ppermute | solution.py:125
  21.1 11.6 %collective-permute-done.8 = f32[8,6144]{1,0:T(8,128)S(1)} collective-permute-done((f32[8,6144]{1,0:T(8,128)S(1)}, f32[8,6144]{1,0:T(8,128)S(1)}, u32[]{:S(2)}, u32[]{:S(2)}) %collective-permute-start.8) | collective-permute-done | bytes 196640 | tf_op jit(solution)/shard_map/ppermute | solution.py:125
  34.0 5.2 %collective-permute-start.11 = (f32[8,6144]{1,0:T(8,128)S(1)}, f32[8,6144]{1,0:T(8,128)S(1)}, u32[]{:S(2)}, u32[]{:S(2)}) collective-permute-start(f32[8,6144]{1,0:T(8,128)S(1)} %get-tuple-element.38), channel_id=1, source_target_pairs={{0,2},{1,3},{2,0},{3,1},{4,6},{5,7},{6,4},{7,5},{8,10},{9,11},{10,... | collective-permute-start | bytes 589832 | tf_op jit(solution)/shard_map/ppermute | solution.py:125
  40.5 12.6 %collective-permute-done.11 = f32[8,6144]{1,0:T(8,128)S(1)} collective-permute-done((f32[8,6144]{1,0:T(8,128)S(1)}, f32[8,6144]{1,0:T(8,128)S(1)}, u32[]{:S(2)}, u32[]{:S(2)}) %collective-permute-start.11) | collective-permute-done | bytes 196640 | tf_op jit(solution)/shard_map/ppermute | solution.py:125
  53.1 1.5 %collective-permute-start.13 = (f32[16,6144]{1,0:T(8,128)S(1)}, f32[16,6144]{1,0:T(8,128)S(1)}, u32[]{:S(2)}, u32[]{:S(2)}) collective-permute-start(f32[16,6144]{1,0:T(8,128)S(1)} %pad_maximum_fusion.2), channel_id=1, source_target_pairs={{0,8},{4,20},{8,0},{12,28},{16,24},{20,4},{24,16},{28,12},{1,9},{5... | collective-permute-start | bytes 1179656 | tf_op jit(solution)/shard_map/ppermute | solution.py:125
  55.2 5.7 %collective-permute-done.13 = f32[16,6144]{1,0:T(8,128)S(1)} collective-permute-done((f32[16,6144]{1,0:T(8,128)S(1)}, f32[16,6144]{1,0:T(8,128)S(1)}, u32[]{:S(2)}, u32[]{:S(2)}) %collective-permute-start.13) | collective-permute-done | bytes 393248 | tf_op jit(solution)/shard_map/ppermute | solution.py:125
  61.5 3.2 %collective-permute-start.21 = (f32[8,4096]{1,0:T(8,128)S(1)}, f32[8,4096]{1,0:T(8,128)S(1)}, u32[]{:S(2)}, u32[]{:S(2)}) collective-permute-start(f32[8,4096]{1,0:T(8,128)S(1)} %get-tuple-element.46), channel_id=1, source_target_pairs={{0,3},{1,2},{2,1},{3,0},{4,7},{5,6},{6,5},{7,4},{8,11},{9,10},{10,... | collective-permute-start | bytes 393224 | tf_op jit(solution)/shard_map/ppermute | solution.py:125
  64.9 1.6 %collective-permute-start.14 = (f32[16,6144]{1,0:T(8,128)S(1)}, f32[16,6144]{1,0:T(8,128)S(1)}, u32[]{:S(2)}, u32[]{:S(2)}) collective-permute-start(f32[16,6144]{1,0:T(8,128)S(1)} %pad_maximum_fusion.1), channel_id=1, source_target_pairs={{0,8},{4,20},{8,0},{12,28},{16,24},{20,4},{24,16},{28,12},{1,9},{5... | collective-permute-start | bytes 1179656 | tf_op jit(solution)/shard_map/ppermute | solution.py:125
  66.4 10.7 %collective-permute-done.15.refs_9_ = f32[32,6144]{1,0:T(8,128)S(1)} collective-permute-done((f32[32,6144]{1,0:T(8,128)S(1)}, f32[32,6144]{1,0:T(8,128)S(1)}, u32[]{:S(2)}, u32[]{:S(2)}) %collective-permute-start.15) | collective-permute-done | bytes 786464 | tf_op jit(solution)/shard_map/ppermute | solution.py:125
  81.0 11.6 %shard_map.28.refs_12_ = f32[704,256]{1,0:T(8,128)S(1)} custom-call(s32[2]{0:T(128)S(1)} %pad_add_fusion.where, f32[704,16384]{1,0:T(8,128)} %v_ref.7, f32[16,16384]{1,0:T(8,128)S(1)} %pad_maximum_fusion.refs_0_, f32[16,16384]{1,0:T(8,128)S(1)} %collective-permute-done.1.refs_1_, f32[16,16384]{1,0:T(8,128)S(1)} %collective-permute-done.2.refs_2_, ...), custom_call_target="tpu_custom_call" | custom-call | flops 19931332608 | bytes 70778880 | tf_op jit(solution)/shard_map/pallas_call | solution.py:93
  94.9 11.4 %shard_map.29.refs_8_.refs_4_ = f32[704,256]{1,0:T(8,128)S(1)} custom-call(s32[2]{0:T(128)S(1)} %pad_add_fusion.where, f32[704,16384]{1,0:T(8,128)} %v_ref.7, f32[16,16384]{1,0:T(8,128)S(1)} %pad_maximum_fusion.refs_0_, f32[16,16384]{1,0:T(8,128)S(1)} %collective-permute-done.1.refs_1_, f32[16,16384]{1,0:T(8,128)S(1)} %collective-permute-done.2.refs_2_, ...), custom_call_target="tpu_custom_call" | custom-call | flops 19931332608 | bytes 70778880 | tf_op jit(solution)/shard_map/pallas_call | solution.py:93
  106.6 7.0 %shard_map.30 = f32[128,768]{1,0:T(8,128)S(1)} custom-call(s32[2]{0:T(128)S(1)} %pad_add_fusion.where, f32[704,16384]{1,0:T(8,128)} %v_ref.7, f32[16,16384]{1,0:T(8,128)S(1)} %pad_maximum_fusion.refs_0_, f32[16,16384]{1,0:T(8,128)S(1)} %collective-permute-done.1.refs_1_, f32[16,16384]{1,0:T(8,128)S(1)} %collective-permute-done.2.refs_2_, ...), custom_call_target="tpu_custom_call" | custom-call | flops 6643777536 | bytes 40894464 | tf_op jit(solution)/shard_map/pallas_call | solution.py:93
  113.7 2.2 %collective-permute-start.28 = (f32[32,768]{1,0:T(8,128)S(1)}, f32[32,768]{1,0:T(8,128)S(1)}, u32[]{:S(2)}, u32[]{:S(2)}) collective-permute-start(f32[32,768]{1,0:T(8,128)S(1)} %get-tuple-element.52), channel_id=1, source_target_pairs={{0,3},{1,2},{2,1},{3,0},{4,7},{5,6},{6,5},{7,4},{8,11},{9,10},{10,... | collective-permute-start | bytes 294920 | tf_op jit(solution)/shard_map/ppermute | solution.py:125
  115.9 7.0 %shard_map.31 = f32[128,768]{1,0:T(8,128)S(1)} custom-call(s32[2]{0:T(128)S(1)} %pad_add_fusion.where, f32[704,16384]{1,0:T(8,128)} %v_ref.7, f32[32,4096]{1,0:T(8,128)S(1)} %constant_dynamic-update-slice_fusion.8.refs_0_, f32[32,4096]{1,0:T(8,128)S(1)} %collective-permute-done.24.refs_1_, f32[32,4096]{1,0:T(8,128)S(1)} %collective-permute-done.25.refs_2_, ...), custom_call_target="tpu_custom_call" | custom-call | flops 6643777536 | bytes 40894464 | tf_op jit(solution)/shard_map/pallas_call | solution.py:93
  125.1 2.0 %collective-permute-start.31 = (f32[32,768]{1,0:T(8,128)S(1)}, f32[32,768]{1,0:T(8,128)S(1)}, u32[]{:S(2)}, u32[]{:S(2)}) collective-permute-start(f32[32,768]{1,0:T(8,128)S(1)} %get-tuple-element.55), channel_id=1, source_target_pairs={{0,2},{1,3},{2,0},{3,1},{4,6},{5,7},{6,4},{7,5},{8,10},{9,11},{10,... | collective-permute-start | bytes 294920 | tf_op jit(solution)/shard_map/ppermute | solution.py:125
  127.0 1.7 %collective-permute-start.32 = (f32[32,768]{1,0:T(8,128)S(1)}, f32[32,768]{1,0:T(8,128)S(1)}, u32[]{:S(2)}, u32[]{:S(2)}) collective-permute-start(f32[32,768]{1,0:T(8,128)S(1)} %get-tuple-element.56), channel_id=1, source_target_pairs={{0,3},{1,2},{2,1},{3,0},{4,7},{5,6},{6,5},{7,4},{8,11},{9,10},{10,... | collective-permute-start | bytes 294920 | tf_op jit(solution)/shard_map/ppermute | solution.py:125
  129.9 1.6 %collective-permute-done.30 = f32[32,768]{1,0:T(8,128)S(1)} collective-permute-done((f32[32,768]{1,0:T(8,128)S(1)}, f32[32,768]{1,0:T(8,128)S(1)}, u32[]{:S(2)}, u32[]{:S(2)}) %collective-permute-start.30) | collective-permute-done | bytes 98336 | tf_op jit(solution)/shard_map/ppermute | solution.py:125
  131.5 4.0 %collective-permute-done.31 = f32[32,768]{1,0:T(8,128)S(1)} collective-permute-done((f32[32,768]{1,0:T(8,128)S(1)}, f32[32,768]{1,0:T(8,128)S(1)}, u32[]{:S(2)}, u32[]{:S(2)}) %collective-permute-start.31) | collective-permute-done | bytes 98336 | tf_op jit(solution)/shard_map/ppermute | solution.py:125
  (73 shorter events, 17.0 us)
Async XLA Ops:
  2.2 10.2 %collective-permute-start = (f32[8,16384]{1,0:T(8,128)S(1)}, f32[8,16384]{1,0:T(8,128)}, u32[]{:S(2)}, u32[]{:S(2)}) collective-permute-start(f32[8,16384]{1,0:T(8,128)S(1)} %get-tuple-element.69), channel_id=1, source_target_pairs={{0,8},{4,20},{8,0},{12,28},{16,24},{20,4},{24,16},{28,12},{1,9},{5... | collective-permute-start | bytes 1572872 | tf_op jit(solution)/shard_map/ppermute | solution.py:125
  5.2 14.4 %collective-permute-start.3 = (f32[8,16384]{1,0:T(8,128)}, f32[8,16384]{1,0:T(8,128)S(1)}, u32[]{:S(2)}, u32[]{:S(2)}) collective-permute-start(f32[8,16384]{1,0:T(8,128)} %get-tuple-element.68), channel_id=1, source_target_pairs={{0,1},{1,0},{2,3},{3,2},{4,5},{5,4},{6,7},{7,6},{8,9},{9,8},{10,11... | collective-permute-start | bytes 1572872 | tf_op jit(solution)/shard_map/ppermute | solution.py:125
  13.5 20.5 %collective-permute-start.1 = (f32[16,16384]{1,0:T(8,128)S(1)}, f32[16,16384]{1,0:T(8,128)S(1)}, u32[]{:S(2)}, u32[]{:S(2)}) collective-permute-start(f32[16,16384]{1,0:T(8,128)S(1)} %pad_maximum_fusion.refs_0_), channel_id=1, source_target_pairs={{0,16},{4,12},{8,24},{12,4},{16,0},{20,28},{24,8},{28,20},{1,17},{... | collective-permute-start | bytes 3145736 | tf_op jit(solution)/shard_map/ppermute | solution.py:125
  15.7 45.8 %collective-permute-start.2 = (f32[16,16384]{1,0:T(8,128)S(1)}, f32[16,16384]{1,0:T(8,128)S(1)}, u32[]{:S(2)}, u32[]{:S(2)}) collective-permute-start(f32[16,16384]{1,0:T(8,128)S(1)} %pad_maximum_fusion.refs_0_), channel_id=1, source_target_pairs={{0,4},{4,0},{8,12},{12,8},{16,20},{20,16},{24,28},{28,24},{1,5},{5... | collective-permute-start | bytes 3145736 | tf_op jit(solution)/shard_map/ppermute | solution.py:125
  15.7 17.0 %collective-permute-start.8 = (f32[8,6144]{1,0:T(8,128)S(1)}, f32[8,6144]{1,0:T(8,128)S(1)}, u32[]{:S(2)}, u32[]{:S(2)}) collective-permute-start(f32[8,6144]{1,0:T(8,128)S(1)} %get-tuple-element.35), channel_id=1, source_target_pairs={{0,2},{1,3},{2,0},{3,1},{4,6},{5,7},{6,4},{7,5},{8,10},{9,11},{10,... | collective-permute-start | bytes 589832 | tf_op jit(solution)/shard_map/ppermute | solution.py:125
  18.2 14.4 %collective-permute-start.9 = (f32[8,6144]{1,0:T(8,128)S(1)}, f32[8,6144]{1,0:T(8,128)S(1)}, u32[]{:S(2)}, u32[]{:S(2)}) collective-permute-start(f32[8,6144]{1,0:T(8,128)S(1)} %get-tuple-element.36), channel_id=1, source_target_pairs={{0,3},{1,2},{2,1},{3,0},{4,7},{5,6},{6,5},{7,4},{8,11},{9,10},{10,... | collective-permute-start | bytes 589832 | tf_op jit(solution)/shard_map/ppermute | solution.py:125
  19.6 13.1 %collective-permute-start.5 = (f32[8,16384]{1,0:T(8,128)S(1)}, f32[8,16384]{1,0:T(8,128)S(1)}, u32[]{:S(2)}, u32[]{:S(2)}) collective-permute-start(f32[8,16384]{1,0:T(8,128)S(1)} %collective-permute-done.3), channel_id=1, source_target_pairs={{0,8},{4,20},{8,0},{12,28},{16,24},{20,4},{24,16},{28,12},{1,9},{5... | collective-permute-start | bytes 1572872 | tf_op jit(solution)/shard_map/ppermute | solution.py:125
  34.0 19.1 %collective-permute-start.11 = (f32[8,6144]{1,0:T(8,128)S(1)}, f32[8,6144]{1,0:T(8,128)S(1)}, u32[]{:S(2)}, u32[]{:S(2)}) collective-permute-start(f32[8,6144]{1,0:T(8,128)S(1)} %get-tuple-element.38), channel_id=1, source_target_pairs={{0,2},{1,3},{2,0},{3,1},{4,6},{5,7},{6,4},{7,5},{8,10},{9,11},{10,... | collective-permute-start | bytes 589832 | tf_op jit(solution)/shard_map/ppermute | solution.py:125
  39.3 15.3 %collective-permute-start.12 = (f32[8,6144]{1,0:T(8,128)S(1)}, f32[8,6144]{1,0:T(8,128)S(1)}, u32[]{:S(2)}, u32[]{:S(2)}) collective-permute-start(f32[8,6144]{1,0:T(8,128)S(1)} %get-tuple-element.39), channel_id=1, source_target_pairs={{0,3},{1,2},{2,1},{3,0},{4,7},{5,6},{6,5},{7,4},{8,11},{9,10},{10,... | collective-permute-start | bytes 589832 | tf_op jit(solution)/shard_map/ppermute | solution.py:125
  39.7 14.9 %collective-permute-start.6 = (f32[16,16384]{1,0:T(8,128)S(1)}, f32[16,16384]{1,0:T(8,128)S(1)}, u32[]{:S(2)}, u32[]{:S(2)}) collective-permute-start(f32[16,16384]{1,0:T(8,128)S(1)} %constant_dynamic-update-slice_fusion.refs_4_), channel_id=1, source_target_pairs={{0,16},{4,12},{8,24},{12,4},{16,0},{20,28},{24,8},{28,20},{1,17},{... | collective-permute-start | bytes 3145736 | tf_op jit(solution)/shard_map/ppermute | solution.py:125
  40.3 21.2 %collective-permute-start.7 = (f32[16,16384]{1,0:T(8,128)S(1)}, f32[16,16384]{1,0:T(8,128)S(1)}, u32[]{:S(2)}, u32[]{:S(2)}) collective-permute-start(f32[16,16384]{1,0:T(8,128)S(1)} %constant_dynamic-update-slice_fusion.refs_4_), channel_id=1, source_target_pairs={{0,4},{4,0},{8,12},{12,8},{16,20},{20,16},{24,28},{28,24},{1,5},{5... | collective-permute-start | bytes 3145736 | tf_op jit(solution)/shard_map/ppermute | solution.py:125
  60.9 16.3 %collective-permute-start.15 = (f32[32,6144]{1,0:T(8,128)S(1)}, f32[32,6144]{1,0:T(8,128)S(1)}, u32[]{:S(2)}, u32[]{:S(2)}) collective-permute-start(f32[32,6144]{1,0:T(8,128)S(1)} %constant_dynamic-update-slice_fusion.5.refs_8_), channel_id=1, source_target_pairs={{0,16},{4,12},{8,24},{12,4},{16,0},{20,28},{24,8},{28,20},{1,17},{... | collective-permute-start | bytes 2359304 | tf_op jit(solution)/shard_map/ppermute | solution.py:125
  61.5 15.6 %collective-permute-start.21 = (f32[8,4096]{1,0:T(8,128)S(1)}, f32[8,4096]{1,0:T(8,128)S(1)}, u32[]{:S(2)}, u32[]{:S(2)}) collective-permute-start(f32[8,4096]{1,0:T(8,128)S(1)} %get-tuple-element.46), channel_id=1, source_target_pairs={{0,3},{1,2},{2,1},{3,0},{4,7},{5,6},{6,5},{7,4},{8,11},{9,10},{10,... | collective-permute-start | bytes 393224 | tf_op jit(solution)/shard_map/ppermute | solution.py:125
  64.8 12.4 %collective-permute-start.20 = (f32[8,4096]{1,0:T(8,128)S(1)}, f32[8,4096]{1,0:T(8,128)S(1)}, u32[]{:S(2)}, u32[]{:S(2)}) collective-permute-start(f32[8,4096]{1,0:T(8,128)S(1)} %get-tuple-element.45), channel_id=1, source_target_pairs={{0,2},{1,3},{2,0},{3,1},{4,6},{5,7},{6,4},{7,5},{8,10},{9,11},{10,... | collective-permute-start | bytes 393224 | tf_op jit(solution)/shard_map/ppermute | solution.py:125
  64.8 14.3 %collective-permute-start.18 = (f32[32,6144]{1,0:T(8,128)S(1)}, f32[32,6144]{1,0:T(8,128)S(1)}, u32[]{:S(2)}, u32[]{:S(2)}) collective-permute-start(f32[32,6144]{1,0:T(8,128)S(1)} %constant_dynamic-update-slice_fusion.5.refs_8_), channel_id=1, source_target_pairs={{0,4},{4,0},{8,12},{12,8},{16,20},{20,16},{24,28},{28,24},{1,5},{5... | collective-permute-start | bytes 2359304 | tf_op jit(solution)/shard_map/ppermute | solution.py:125
  64.9 12.4 %collective-permute-start.14 = (f32[16,6144]{1,0:T(8,128)S(1)}, f32[16,6144]{1,0:T(8,128)S(1)}, u32[]{:S(2)}, u32[]{:S(2)}) collective-permute-start(f32[16,6144]{1,0:T(8,128)S(1)} %pad_maximum_fusion.1), channel_id=1, source_target_pairs={{0,8},{4,20},{8,0},{12,28},{16,24},{20,4},{24,16},{28,12},{1,9},{5... | collective-permute-start | bytes 1179656 | tf_op jit(solution)/shard_map/ppermute | solution.py:125
  77.3 15.3 %collective-permute-start.16 = (f32[32,6144]{1,0:T(8,128)S(1)}, f32[32,6144]{1,0:T(8,128)S(1)}, u32[]{:S(2)}, u32[]{:S(2)}) collective-permute-start(f32[32,6144]{1,0:T(8,128)S(1)} %constant_dynamic-update-slice_fusion.2.refs_8_), channel_id=1, source_target_pairs={{0,16},{4,12},{8,24},{12,4},{16,0},{20,28},{24,8},{28,20},{1,17},{... | collective-permute-start | bytes 2359304 | tf_op jit(solution)/shard_map/ppermute | solution.py:125
  77.9 16.1 %collective-permute-start.17 = (f32[32,6144]{1,0:T(8,128)S(1)}, f32[32,6144]{1,0:T(8,128)S(1)}, u32[]{:S(2)}, u32[]{:S(2)}) collective-permute-start(f32[32,6144]{1,0:T(8,128)S(1)} %constant_dynamic-update-slice_fusion.2.refs_8_), channel_id=1, source_target_pairs={{0,4},{4,0},{8,12},{12,8},{16,20},{20,16},{24,28},{28,24},{1,5},{5... | collective-permute-start | bytes 2359304 | tf_op jit(solution)/shard_map/ppermute | solution.py:125
  79.5 13.1 %collective-permute-start.22 = (f32[16,4096]{1,0:T(8,128)S(1)}, f32[16,4096]{1,0:T(8,128)S(1)}, u32[]{:S(2)}, u32[]{:S(2)}) collective-permute-start(f32[16,4096]{1,0:T(8,128)S(1)} %pad_maximum_fusion.3), channel_id=1, source_target_pairs={{0,8},{4,20},{8,0},{12,28},{16,24},{20,4},{24,16},{28,12},{1,9},{5... | collective-permute-start | bytes 786440 | tf_op jit(solution)/shard_map/ppermute | solution.py:125
  92.7 13.7 %collective-permute-start.24 = (f32[32,4096]{1,0:T(8,128)S(1)}, f32[32,4096]{1,0:T(8,128)S(1)}, u32[]{:S(2)}, u32[]{:S(2)}) collective-permute-start(f32[32,4096]{1,0:T(8,128)S(1)} %constant_dynamic-update-slice_fusion.8.refs_0_), channel_id=1, source_target_pairs={{0,16},{4,12},{8,24},{12,4},{16,0},{20,28},{24,8},{28,20},{1,17},{... | collective-permute-start | bytes 1572872 | tf_op jit(solution)/shard_map/ppermute | solution.py:125
  93.3 20.4 %collective-permute-start.25 = (f32[32,4096]{1,0:T(8,128)S(1)}, f32[32,4096]{1,0:T(8,128)S(1)}, u32[]{:S(2)}, u32[]{:S(2)}) collective-permute-start(f32[32,4096]{1,0:T(8,128)S(1)} %constant_dynamic-update-slice_fusion.8.refs_0_), channel_id=1, source_target_pairs={{0,4},{4,0},{8,12},{12,8},{16,20},{20,16},{24,28},{28,24},{1,5},{5... | collective-permute-start | bytes 1572872 | tf_op jit(solution)/shard_map/ppermute | solution.py:125
  113.7 13.4 %collective-permute-start.27 = (f32[32,768]{1,0:T(8,128)S(1)}, f32[32,768]{1,0:T(8,128)S(1)}, u32[]{:S(2)}, u32[]{:S(2)}) collective-permute-start(f32[32,768]{1,0:T(8,128)S(1)} %get-tuple-element.51), channel_id=1, source_target_pairs={{0,2},{1,3},{2,0},{3,1},{4,6},{5,7},{6,4},{7,5},{8,10},{9,11},{10,... | collective-permute-start | bytes 294920 | tf_op jit(solution)/shard_map/ppermute | solution.py:125
  113.7 15.0 %collective-permute-start.28 = (f32[32,768]{1,0:T(8,128)S(1)}, f32[32,768]{1,0:T(8,128)S(1)}, u32[]{:S(2)}, u32[]{:S(2)}) collective-permute-start(f32[32,768]{1,0:T(8,128)S(1)} %get-tuple-element.52), channel_id=1, source_target_pairs={{0,3},{1,2},{2,1},{3,0},{4,7},{5,6},{6,5},{7,4},{8,11},{9,10},{10,... | collective-permute-start | bytes 294920 | tf_op jit(solution)/shard_map/ppermute | solution.py:125
  125.1 10.4 %collective-permute-start.31 = (f32[32,768]{1,0:T(8,128)S(1)}, f32[32,768]{1,0:T(8,128)S(1)}, u32[]{:S(2)}, u32[]{:S(2)}) collective-permute-start(f32[32,768]{1,0:T(8,128)S(1)} %get-tuple-element.55), channel_id=1, source_target_pairs={{0,2},{1,3},{2,0},{3,1},{4,6},{5,7},{6,4},{7,5},{8,10},{9,11},{10,... | collective-permute-start | bytes 294920 | tf_op jit(solution)/shard_map/ppermute | solution.py:125
  (10 other events, 62.8 us)

commit v3 on v2

--- a/solution.py
+++ b/solution.py
@@ -12,7 +12,7 @@
 SUB, LANE, MXU = 8, 128, 256
 
 PARTS = (3, 3, 2)
-TILE, LIMIT = 2048, 28
+TILE, LIMIT = 2048, 22
 COST = 3
 
 
@@ -32,7 +32,7 @@
     return dot(vh, th) + (dot(vh, tl) + dot(vl, th))
 
 
-def kernel(where, v_ref, *refs, groups, lanes, acc, last):
+def kernel(where, v_ref, *refs, groups, lanes, acc, last, tile, skips, held):
     step = pl.program_id(0)
     if last:
         out_ref, tau, total = refs[-3:]
@@ -48,8 +48,10 @@
                 at = half * 16 * lanes + ((source * 2 + its) * 2 + begin) * lanes
                 size = planes * lanes
                 ref = refs[4 * g + 2 * other + m // 2]
-                tau[pl.ds(pl.multiple_of(at, lanes), size), :] = ref[pl.ds(m % 2 * size, size), :]
-    new = product(v_ref[...], tau[...])
+                here = pl.ds(pl.multiple_of(skips[g] + step * tile, tile), tile)
+                tau[pl.ds(pl.multiple_of(at, lanes), size), :] = ref[pl.ds(m % 2 * size, size), here]
+    v = v_ref[:, pl.ds(pl.multiple_of(step * tile, tile), tile)] if held else v_ref[...]
+    new = product(v, tau[...])
 
     @pl.when(step == 0)
     def _():
@@ -69,20 +71,24 @@
                 out_ref[:, rows:] = jnp.zeros((out_ref.shape[0], out_ref.shape[1] - rows), F32)
 
 
-def multiply(where, v, quads, acc, at, width, tile, lanes, last):
+def multiply(where, v, quads, acc, at, width, tile, lanes, last, held):
     rows = v.shape[0]
     groups = tuple(q[0] for q in quads)
     ij = len({g[0] for g in groups}) * 16 * lanes
     lowest = min(g[0] for g in groups)
     groups = tuple((half - lowest, begin, planes) for half, begin, planes in groups)
-    specs, operands = [pl.BlockSpec((rows, tile), lambda i, w: (0, i + at // tile))], [v]
-    for _, pieces, begin in quads:
+    if held:
+        specs, operands = [pl.BlockSpec(memory_space=pltpu.VMEM)], [v]
+    else:
+        specs, operands = [pl.BlockSpec((rows, tile), lambda i, w: (0, i + at // tile))], [v]
+    for _, pieces, _ in quads:
         for a in pieces:
-            specs.append(pl.BlockSpec((a.shape[0], tile), lambda i, w, b=begin: (0, i + (at - b) // tile)))
-            operands.append(a)
+            specs.append(pl.BlockSpec(memory_space=pltpu.VMEM))
+            operands.append(pltpu.with_memory_space_constraint(a, pltpu.VMEM))
     if acc is not None:
         specs.append(pl.BlockSpec((rows, ij), lambda i, w: (0, acc[1])))
         operands.append(acc[0])
+    skips = tuple(at - begin for _, _, begin in quads)
     scratch = [pltpu.VMEM((ij, tile), F32)]
     if last:
         shape = (ij, pl.cdiv(rows, LANE) * LANE)
@@ -91,7 +97,7 @@
     else:
         shape, spec = (rows, ij), pl.BlockSpec((rows, ij), lambda i, w: (0, 0))
     return pl.pallas_call(
-        functools.partial(kernel, groups=groups, lanes=lanes, acc=acc is not None, last=last),
+        functools.partial(kernel, groups=groups, lanes=lanes, acc=acc is not None, last=last, tile=tile, skips=skips, held=held),
         grid_spec=pltpu.PrefetchScalarGridSpec(
             num_scalar_prefetch=1, grid=(width // tile,), in_specs=specs, out_specs=spec, scratch_shapes=scratch
         ),
@@ -119,6 +125,7 @@
     begins = [sum(parts[:i]) for i in range(len(parts) + 1)]
     seen = []
     piece, first, pair, both, their_pair, their_both, gone = {}, {}, {}, {}, {}, {}, {}
+    held = {}
     totals, sums = [None, None], [None, None]
 
     def send(x, axis, pairs):
@@ -149,6 +156,13 @@
 
     def have(u):
         return pair[u], both[u], their_pair[u], their_both[u]
+
+    def hold(u):
+        begin = begins[u - 2]
+        v = lax.optimization_barrier((integrals, *seen))[0]
+        v = lax.slice(v, (0, begin), (height, begin + parts[u - 2]))
+        held[begin] = pltpu.with_memory_space_constraint(v, pltpu.VMEM)
+        seen.append(held[begin])
 
     def times(halves, begin, width):
         quads = []
@@ -158,7 +172,10 @@
             u = begins.index(begin) + 2
             quads.append(((1, 0, 2), have(u), begin))
         last = begin + width == block
-        acc = multiply(where, integrals, quads, totals[halves[0]], begin, width, TILE, lanes, last)
+        v = held.get(begin)
+        acc = multiply(
+            where, integrals if v is None else v, quads, totals[halves[0]], begin, width, TILE, lanes, last, v is not None
+        )
         for place, half in enumerate(halves):
             totals[half] = (acc, place)
         seen.append(acc)
@@ -178,6 +195,7 @@
     along(2)
     seen.extend(gone[1])
     to_near(1)
+    hold(4)
     seen.append(both[0])
     swap_both(0)
     seen.append(first[1])
@@ -185,6 +203,7 @@
     swap_pair(1)
     seen.extend(gone[2])
     to_near(2)
+    seen.append(their_pair[1])
     along(3)
     seen.append(both[1])
     swap_both(1)

time: 136 us -> 132 us (0.971)
  waiting for transfers between devices: 55.5 us -> 40.6 us
  local copies, waits for them, and re-layouts: 3.29 us -> 13.3 us
  starting transfers between devices: 38.9 us -> 44.5 us
  Pallas kernels: 37 us -> 31.8 us
    ppermute x33, waiting for transfers between devices: 55.5 us -> 40.6 us  [send(): return lax.ppermute(lax.optimization_barrier((x, *seen))[0], axis, pairs)]
    slice x0 -> x1, local copies, waits for them, and re-layouts: none -> 9.97 us  [hold(): v = lax.slice(v, (0, begin), (height, begin + parts[u - 2]))]
    ppermute x33, starting transfers between devices: 38.9 us -> 44.5 us  [send(): return lax.ppermute(lax.optimization_barrier((x, *seen))[0], axis, pairs)]
    pallas_call x4, Pallas kernels: 37 us -> 31.8 us  [multiply(): pl.pallas_call(functools.partial(kernel, groups=groups, lanes=lanes, acc=...]
  transfers between devices with their start and end apart: 33 -> 33, of which waited for: 11 -> 14; matrix products, arithmetic and copies ran while one was open for 1% -> 9% of each run, Pallas kernels for 27% -> 24%
where the time goes in v3:
time: 132 us
  starting transfers between devices  44.5 us (34%)
  waiting for transfers between devices  40.6 us (31%)
  Pallas kernels  31.8 us (24%)
  local copies, waits for them, and re-layouts  13.3 us (10%)
  other arithmetic  1.34 us (1%)
    ppermute x33, starting transfers between devices, send(): return lax.ppermute(lax.optimization_barrier((x, *seen))[0], axis, pairs)  44.5 us
    ppermute x33, waiting for transfers between devices, send(): return lax.ppermute(lax.optimization_barrier((x, *seen))[0], axis, pairs)  40.6 us
    pallas_call x4, Pallas kernels, multiply(): pl.pallas_call(functools.partial(kernel, groups=groups, lanes=lanes, acc=...  31.8 us
    slice x1, local copies, waits for them, and re-layouts, hold(): v = lax.slice(v, (0, begin), (height, begin + parts[u - 2]))  9.97 us
  transfers between devices with their start and end apart: 33, of which 14 were waited for; matrix products, arithmetic and copies ran while one was open for 9% of the time, Pallas kernels for 24%

profile of v3, /device:TPU:0, one launch (start us, length us, event | category | flops | bytes accessed | tf_op | source)
XLA Modules:
  0.0 131.9 jit_solution(16994155092595152813)
XLA Ops:
  0.0 2.2 %dynamic-slice_bitcast_fusion = (f32[8,16384]{1,0:T(8,128)}, f32[8,16384]{1,0:T(8,128)S(1)}) fusion(f32[65536,8]{0,1:T(8,128)} %param.2, s32[]{:T(128)S(6)} %select_n.106, s32[]{:T(128)S(6)} %select_n.105), kind=kLoop, calls=%fused_computation.1 | loop fusion | bytes 2097160 | tf_op jit(solution)/shard_map/dynamic_slice | solution.py:135
  2.2 2.9 %collective-permute-start = (f32[8,16384]{1,0:T(8,128)S(1)}, f32[8,16384]{1,0:T(8,128)}, u32[]{:S(2)}, u32[]{:S(2)}) collective-permute-start(f32[8,16384]{1,0:T(8,128)S(1)} %get-tuple-element.71), channel_id=1, source_target_pairs={{0,8},{4,20},{8,0},{12,28},{16,24},{20,4},{24,16},{28,12},{1,9},{5... | collective-permute-start | bytes 1572872 | tf_op jit(solution)/shard_map/ppermute | solution.py:132
  6.9 5.5 %collective-permute-done = f32[8,16384]{1,0:T(8,128)} collective-permute-done((f32[8,16384]{1,0:T(8,128)S(1)}, f32[8,16384]{1,0:T(8,128)}, u32[]{:S(2)}, u32[]{:S(2)}) %collective-permute-start) | collective-permute-done | bytes 524320 | tf_op jit(solution)/shard_map/ppermute | solution.py:132
  13.5 2.1 %collective-permute-start.2 = (f32[16,16384]{1,0:T(8,128)S(1)}, f32[16,16384]{1,0:T(8,128)S(1)}, u32[]{:S(2)}, u32[]{:S(2)}) collective-permute-start(f32[16,16384]{1,0:T(8,128)S(1)} %pad_maximum_fusion.refs_0_), channel_id=1, source_target_pairs={{0,16},{4,12},{8,24},{12,4},{16,0},{20,28},{24,8},{28,20},{1,17},{... | collective-permute-start | bytes 3145736 | tf_op jit(solution)/shard_map/ppermute | solution.py:132
  15.7 3.1 %collective-permute-done.1 = f32[8,16384]{1,0:T(8,128)S(1)} collective-permute-done((f32[8,16384]{1,0:T(8,128)}, f32[8,16384]{1,0:T(8,128)S(1)}, u32[]{:S(2)}, u32[]{:S(2)}) %collective-permute-start.1) | collective-permute-done | bytes 524320 | tf_op jit(solution)/shard_map/ppermute | solution.py:132
  20.2 2.6 %collective-permute-start.8 = (f32[8,6144]{1,0:T(8,128)S(1)}, f32[8,6144]{1,0:T(8,128)S(1)}, u32[]{:S(2)}, u32[]{:S(2)}) collective-permute-start(f32[8,6144]{1,0:T(8,128)S(1)} %get-tuple-element.37), channel_id=1, source_target_pairs={{0,2},{1,3},{2,0},{3,1},{4,6},{5,7},{6,4},{7,5},{8,10},{9,11},{10,... | collective-permute-start | bytes 589832 | tf_op jit(solution)/shard_map/ppermute | solution.py:132
  24.3 10.0 %slice.54.v_ref = f32[704,4096]{1,0:T(8,128)} slice(f32[704,16384]{1,0:T(8,128)} %v_ref.3), slice={[0:704], [12288:16384]} | slice | bytes 23068672 | tf_op jit(solution)/shard_map/slice | solution.py:163
  38.7 6.5 %collective-permute-start.11 = (f32[8,6144]{1,0:T(8,128)S(1)}, f32[8,6144]{1,0:T(8,128)S(1)}, u32[]{:S(2)}, u32[]{:S(2)}) collective-permute-start(f32[8,6144]{1,0:T(8,128)S(1)} %get-tuple-element.40), channel_id=1, source_target_pairs={{0,2},{1,3},{2,0},{3,1},{4,6},{5,7},{6,4},{7,5},{8,10},{9,11},{10,... | collective-permute-start | bytes 589832 | tf_op jit(solution)/shard_map/ppermute | solution.py:132
  45.2 3.6 %collective-permute-done.13 = f32[16,6144]{1,0:T(8,128)S(1)} collective-permute-done((f32[16,6144]{1,0:T(8,128)S(1)}, f32[16,6144]{1,0:T(8,128)S(1)}, u32[]{:S(2)}, u32[]{:S(2)}) %collective-permute-start.13) | collective-permute-done | bytes 393248 | tf_op jit(solution)/shard_map/ppermute | solution.py:132
  48.8 3.0 %collective-permute-start.12 = (f32[8,6144]{1,0:T(8,128)S(1)}, f32[8,6144]{1,0:T(8,128)S(1)}, u32[]{:S(2)}, u32[]{:S(2)}) collective-permute-start(f32[8,6144]{1,0:T(8,128)S(1)} %get-tuple-element.41), channel_id=1, source_target_pairs={{0,3},{1,2},{2,1},{3,0},{4,7},{5,6},{6,5},{7,4},{8,11},{9,10},{10,... | collective-permute-start | bytes 589832 | tf_op jit(solution)/shard_map/ppermute | solution.py:132
  51.8 2.2 %collective-permute-done.6.refs_5_ = f32[16,16384]{1,0:T(8,128)S(1)} collective-permute-done((f32[16,16384]{1,0:T(8,128)S(1)}, f32[16,16384]{1,0:T(8,128)S(1)}, u32[]{:S(2)}, u32[]{:S(2)}) %collective-permute-start.6) | collective-permute-done | bytes 1048608 | tf_op jit(solution)/shard_map/ppermute | solution.py:132
  55.8 3.6 %collective-permute-done.11 = f32[8,6144]{1,0:T(8,128)S(1)} collective-permute-done((f32[8,6144]{1,0:T(8,128)S(1)}, f32[8,6144]{1,0:T(8,128)S(1)}, u32[]{:S(2)}, u32[]{:S(2)}) %collective-permute-start.11) | collective-permute-done | bytes 196640 | tf_op jit(solution)/shard_map/ppermute | solution.py:132
  60.0 3.2 %collective-permute-done.10.refs_7_ = f32[16,16384]{1,0:T(8,128)S(1)} collective-permute-done((f32[16,16384]{1,0:T(8,128)S(1)}, f32[16,16384]{1,0:T(8,128)S(1)}, u32[]{:S(2)}, u32[]{:S(2)}) %collective-permute-start.10) | collective-permute-done | bytes 1048608 | tf_op jit(solution)/shard_map/ppermute | solution.py:132
  63.2 4.8 %collective-permute-start.20 = (f32[8,4096]{1,0:T(8,128)S(1)}, f32[8,4096]{1,0:T(8,128)S(1)}, u32[]{:S(2)}, u32[]{:S(2)}) collective-permute-start(f32[8,4096]{1,0:T(8,128)S(1)} %get-tuple-element.47), channel_id=1, source_target_pairs={{0,2},{1,3},{2,0},{3,1},{4,6},{5,7},{6,4},{7,5},{8,10},{9,11},{10,... | collective-permute-start | bytes 393224 | tf_op jit(solution)/shard_map/ppermute | solution.py:132
  68.4 3.0 %collective-permute-done.21 = f32[8,4096]{1,0:T(8,128)S(1)} collective-permute-done((f32[8,4096]{1,0:T(8,128)S(1)}, f32[8,4096]{1,0:T(8,128)S(1)}, u32[]{:S(2)}, u32[]{:S(2)}) %collective-permute-start.21) | collective-permute-done | bytes 131104 | tf_op jit(solution)/shard_map/ppermute | solution.py:132
  71.4 7.5 %collective-permute-done.20 = f32[8,4096]{1,0:T(8,128)S(1)} collective-permute-done((f32[8,4096]{1,0:T(8,128)S(1)}, f32[8,4096]{1,0:T(8,128)S(1)}, u32[]{:S(2)}, u32[]{:S(2)}) %collective-permute-start.20) | collective-permute-done | bytes 131104 | tf_op jit(solution)/shard_map/ppermute | solution.py:132
  79.3 2.0 %collective-permute-start.22 = (f32[16,4096]{1,0:T(8,128)S(1)}, f32[16,4096]{1,0:T(8,128)S(1)}, u32[]{:S(2)}, u32[]{:S(2)}) collective-permute-start(f32[16,4096]{1,0:T(8,128)S(1)} %pad_maximum_fusion.3), channel_id=1, source_target_pairs={{0,8},{4,20},{8,0},{12,28},{16,24},{20,4},{24,16},{28,12},{1,9},{5... | collective-permute-start | bytes 786440 | tf_op jit(solution)/shard_map/ppermute | solution.py:132
  81.4 11.4 %shard_map.28.refs_12_ = f32[704,256]{1,0:T(8,128)S(1)} custom-call(s32[2]{0:T(128)S(1)} %pad_add_fusion.where, f32[704,16384]{1,0:T(8,128)} %v_ref.3, f32[16,16384]{1,0:T(8,128)S(1)} %pad_maximum_fusion.refs_0_, f32[16,16384]{1,0:T(8,128)S(1)} %collective-permute-done.2.refs_1_, f32[16,16384]{1,0:T(8,128)S(1)} %collective-permute-done.3.refs_2_, ...), custom_call_target="tpu_custom_call" | custom-call | flops 19931332608 | bytes 70778880 | tf_op jit(solution)/shard_map/pallas_call | solution.py:99
  96.0 11.7 %shard_map.29.refs_8_.refs_4_ = f32[704,256]{1,0:T(8,128)S(1)} custom-call(s32[2]{0:T(128)S(1)} %pad_add_fusion.where, f32[704,16384]{1,0:T(8,128)} %v_ref.3, f32[16,16384]{1,0:T(8,128)S(1)} %pad_maximum_fusion.refs_0_, f32[16,16384]{1,0:T(8,128)S(1)} %collective-permute-done.2.refs_1_, f32[16,16384]{1,0:T(8,128)S(1)} %collective-permute-done.3.refs_2_, ...), custom_call_target="tpu_custom_call" | custom-call | flops 19931332608 | bytes 70778880 | tf_op jit(solution)/shard_map/pallas_call | solution.py:99
  108.2 4.4 %shard_map.30 = f32[128,768]{1,0:T(8,128)S(1)} custom-call(s32[2]{0:T(128)S(1)} %pad_add_fusion.where, f32[704,4096]{1,0:T(8,128)S(1)} %bitcast.30, f32[16,16384]{1,0:T(8,128)S(1)} %pad_maximum_fusion.refs_0_, f32[16,16384]{1,0:T(8,128)S(1)} %collective-permute-done.2.refs_1_, f32[16,16384]{1,0:T(8,128)S(1)} %collective-permute-done.3.refs_2_, ...), custom_call_target="tpu_custom_call" | custom-call | flops 6643777536 | bytes 40894464 | tf_op jit(solution)/shard_map/pallas_call | solution.py:99
  113.3 4.4 %shard_map.31 = f32[128,768]{1,0:T(8,128)S(1)} custom-call(s32[2]{0:T(128)S(1)} %pad_add_fusion.where, f32[704,4096]{1,0:T(8,128)S(1)} %bitcast.30, f32[32,4096]{1,0:T(8,128)S(1)} %constant_dynamic-update-slice_fusion.8.refs_0_, f32[32,4096]{1,0:T(8,128)S(1)} %collective-permute-done.24.refs_1_, f32[32,4096]{1,0:T(8,128)S(1)} %collective-permute-done.25.refs_2_, ...), custom_call_target="tpu_custom_call" | custom-call | flops 6643777536 | bytes 40894464 | tf_op jit(solution)/shard_map/pallas_call | solution.py:99
  117.7 3.0 %collective-permute-start.29 = (f32[32,768]{1,0:T(8,128)S(1)}, f32[32,768]{1,0:T(8,128)S(1)}, u32[]{:S(2)}, u32[]{:S(2)}) collective-permute-start(f32[32,768]{1,0:T(8,128)S(1)} %get-tuple-element.55), channel_id=1, source_target_pairs={{0,1},{1,0},{2,3},{3,2},{4,5},{5,4},{6,7},{7,6},{8,9},{9,8},{10,11... | collective-permute-start | bytes 294920 | tf_op jit(solution)/shard_map/ppermute | solution.py:132
  122.2 2.9 %collective-permute-start.32 = (f32[32,768]{1,0:T(8,128)S(1)}, f32[32,768]{1,0:T(8,128)S(1)}, u32[]{:S(2)}, u32[]{:S(2)}) collective-permute-start(f32[32,768]{1,0:T(8,128)S(1)} %get-tuple-element.58), channel_id=1, source_target_pairs={{0,3},{1,2},{2,1},{3,0},{4,7},{5,6},{6,5},{7,4},{8,11},{9,10},{10,... | collective-permute-start | bytes 294920 | tf_op jit(solution)/shard_map/ppermute | solution.py:132
  127.0 4.0 %collective-permute-done.31 = f32[32,768]{1,0:T(8,128)S(1)} collective-permute-done((f32[32,768]{1,0:T(8,128)S(1)}, f32[32,768]{1,0:T(8,128)S(1)}, u32[]{:S(2)}, u32[]{:S(2)}) %collective-permute-start.31) | collective-permute-done | bytes 98336 | tf_op jit(solution)/shard_map/ppermute | solution.py:132
  (81 shorter events, 21.7 us)
Async XLA Ops:
  2.2 10.2 %collective-permute-start = (f32[8,16384]{1,0:T(8,128)S(1)}, f32[8,16384]{1,0:T(8,128)}, u32[]{:S(2)}, u32[]{:S(2)}) collective-permute-start(f32[8,16384]{1,0:T(8,128)S(1)} %get-tuple-element.71), channel_id=1, source_target_pairs={{0,8},{4,20},{8,0},{12,28},{16,24},{20,4},{24,16},{28,12},{1,9},{5... | collective-permute-start | bytes 1572872 | tf_op jit(solution)/shard_map/ppermute | solution.py:132
  5.2 13.6 %collective-permute-start.1 = (f32[8,16384]{1,0:T(8,128)}, f32[8,16384]{1,0:T(8,128)S(1)}, u32[]{:S(2)}, u32[]{:S(2)}) collective-permute-start(f32[8,16384]{1,0:T(8,128)} %get-tuple-element.70), channel_id=1, source_target_pairs={{0,1},{1,0},{2,3},{3,2},{4,5},{5,4},{6,7},{7,6},{8,9},{9,8},{10,11... | collective-permute-start | bytes 1572872 | tf_op jit(solution)/shard_map/ppermute | solution.py:132
  13.5 21.3 %collective-permute-start.2 = (f32[16,16384]{1,0:T(8,128)S(1)}, f32[16,16384]{1,0:T(8,128)S(1)}, u32[]{:S(2)}, u32[]{:S(2)}) collective-permute-start(f32[16,16384]{1,0:T(8,128)S(1)} %pad_maximum_fusion.refs_0_), channel_id=1, source_target_pairs={{0,16},{4,12},{8,24},{12,4},{16,0},{20,28},{24,8},{28,20},{1,17},{... | collective-permute-start | bytes 3145736 | tf_op jit(solution)/shard_map/ppermute | solution.py:132
  15.7 44.3 %collective-permute-start.3 = (f32[16,16384]{1,0:T(8,128)S(1)}, f32[16,16384]{1,0:T(8,128)S(1)}, u32[]{:S(2)}, u32[]{:S(2)}) collective-permute-start(f32[16,16384]{1,0:T(8,128)S(1)} %pad_maximum_fusion.refs_0_), channel_id=1, source_target_pairs={{0,4},{4,0},{8,12},{12,8},{16,20},{20,16},{24,28},{28,24},{1,5},{5... | collective-permute-start | bytes 3145736 | tf_op jit(solution)/shard_map/ppermute | solution.py:132
  18.8 16.0 %collective-permute-start.5 = (f32[8,16384]{1,0:T(8,128)S(1)}, f32[8,16384]{1,0:T(8,128)S(1)}, u32[]{:S(2)}, u32[]{:S(2)}) collective-permute-start(f32[8,16384]{1,0:T(8,128)S(1)} %collective-permute-done.1), channel_id=1, source_target_pairs={{0,8},{4,20},{8,0},{12,28},{16,24},{20,4},{24,16},{28,12},{1,9},{5... | collective-permute-start | bytes 1572872 | tf_op jit(solution)/shard_map/ppermute | solution.py:132
  20.2 14.5 %collective-permute-start.8 = (f32[8,6144]{1,0:T(8,128)S(1)}, f32[8,6144]{1,0:T(8,128)S(1)}, u32[]{:S(2)}, u32[]{:S(2)}) collective-permute-start(f32[8,6144]{1,0:T(8,128)S(1)} %get-tuple-element.37), channel_id=1, source_target_pairs={{0,2},{1,3},{2,0},{3,1},{4,6},{5,7},{6,4},{7,5},{8,10},{9,11},{10,... | collective-permute-start | bytes 589832 | tf_op jit(solution)/shard_map/ppermute | solution.py:132
  22.9 11.9 %collective-permute-start.9 = (f32[8,6144]{1,0:T(8,128)S(1)}, f32[8,6144]{1,0:T(8,128)S(1)}, u32[]{:S(2)}, u32[]{:S(2)}) collective-permute-start(f32[8,6144]{1,0:T(8,128)S(1)} %get-tuple-element.38), channel_id=1, source_target_pairs={{0,3},{1,2},{2,1},{3,0},{4,7},{5,6},{6,5},{7,4},{8,11},{9,10},{10,... | collective-permute-start | bytes 589832 | tf_op jit(solution)/shard_map/ppermute | solution.py:132
  35.0 19.1 %collective-permute-start.6 = (f32[16,16384]{1,0:T(8,128)S(1)}, f32[16,16384]{1,0:T(8,128)S(1)}, u32[]{:S(2)}, u32[]{:S(2)}) collective-permute-start(f32[16,16384]{1,0:T(8,128)S(1)} %constant_dynamic-update-slice_fusion.refs_4_), channel_id=1, source_target_pairs={{0,16},{4,12},{8,24},{12,4},{16,0},{20,28},{24,8},{28,20},{1,17},{... | collective-permute-start | bytes 3145736 | tf_op jit(solution)/shard_map/ppermute | solution.py:132
  36.8 12.0 %collective-permute-start.13 = (f32[16,6144]{1,0:T(8,128)S(1)}, f32[16,6144]{1,0:T(8,128)S(1)}, u32[]{:S(2)}, u32[]{:S(2)}) collective-permute-start(f32[16,6144]{1,0:T(8,128)S(1)} %pad_maximum_fusion.2), channel_id=1, source_target_pairs={{0,8},{4,20},{8,0},{12,28},{16,24},{20,4},{24,16},{28,12},{1,9},{5... | collective-permute-start | bytes 1179656 | tf_op jit(solution)/shard_map/ppermute | solution.py:132
  38.6 21.3 %collective-permute-start.4 = (f32[16,16384]{1,0:T(8,128)S(1)}, f32[16,16384]{1,0:T(8,128)S(1)}, u32[]{:S(2)}, u32[]{:S(2)}) collective-permute-start(f32[16,16384]{1,0:T(8,128)S(1)} %collective-permute-done.2.refs_1_), channel_id=1, source_target_pairs={{0,4},{4,0},{8,12},{12,8},{16,20},{20,16},{24,28},{28,24},{1,5},{5... | collective-permute-start | bytes 3145736 | tf_op jit(solution)/shard_map/ppermute | solution.py:132
  38.7 20.7 %collective-permute-start.11 = (f32[8,6144]{1,0:T(8,128)S(1)}, f32[8,6144]{1,0:T(8,128)S(1)}, u32[]{:S(2)}, u32[]{:S(2)}) collective-permute-start(f32[8,6144]{1,0:T(8,128)S(1)} %get-tuple-element.40), channel_id=1, source_target_pairs={{0,2},{1,3},{2,0},{3,1},{4,6},{5,7},{6,4},{7,5},{8,10},{9,11},{10,... | collective-permute-start | bytes 589832 | tf_op jit(solution)/shard_map/ppermute | solution.py:132
  48.8 10.6 %collective-permute-start.12 = (f32[8,6144]{1,0:T(8,128)S(1)}, f32[8,6144]{1,0:T(8,128)S(1)}, u32[]{:S(2)}, u32[]{:S(2)}) collective-permute-start(f32[8,6144]{1,0:T(8,128)S(1)} %get-tuple-element.41), channel_id=1, source_target_pairs={{0,3},{1,2},{2,1},{3,0},{4,7},{5,6},{6,5},{7,4},{8,11},{9,10},{10,... | collective-permute-start | bytes 589832 | tf_op jit(solution)/shard_map/ppermute | solution.py:132
  54.1 14.4 %collective-permute-start.15 = (f32[32,6144]{1,0:T(8,128)S(1)}, f32[32,6144]{1,0:T(8,128)S(1)}, u32[]{:S(2)}, u32[]{:S(2)}) collective-permute-start(f32[32,6144]{1,0:T(8,128)S(1)} %constant_dynamic-update-slice_fusion.5.refs_8_), channel_id=1, source_target_pairs={{0,16},{4,12},{8,24},{12,4},{16,0},{20,28},{24,8},{28,20},{1,17},{... | collective-permute-start | bytes 2359304 | tf_op jit(solution)/shard_map/ppermute | solution.py:132
  59.4 19.9 %collective-permute-start.18 = (f32[32,6144]{1,0:T(8,128)S(1)}, f32[32,6144]{1,0:T(8,128)S(1)}, u32[]{:S(2)}, u32[]{:S(2)}) collective-permute-start(f32[32,6144]{1,0:T(8,128)S(1)} %constant_dynamic-update-slice_fusion.5.refs_8_), channel_id=1, source_target_pairs={{0,4},{4,0},{8,12},{12,8},{16,20},{20,16},{24,28},{28,24},{1,5},{5... | collective-permute-start | bytes 2359304 | tf_op jit(solution)/shard_map/ppermute | solution.py:132
  63.2 15.8 %collective-permute-start.20 = (f32[8,4096]{1,0:T(8,128)S(1)}, f32[8,4096]{1,0:T(8,128)S(1)}, u32[]{:S(2)}, u32[]{:S(2)}) collective-permute-start(f32[8,4096]{1,0:T(8,128)S(1)} %get-tuple-element.47), channel_id=1, source_target_pairs={{0,2},{1,3},{2,0},{3,1},{4,6},{5,7},{6,4},{7,5},{8,10},{9,11},{10,... | collective-permute-start | bytes 393224 | tf_op jit(solution)/shard_map/ppermute | solution.py:132
  68.0 10.9 %collective-permute-start.14 = (f32[16,6144]{1,0:T(8,128)S(1)}, f32[16,6144]{1,0:T(8,128)S(1)}, u32[]{:S(2)}, u32[]{:S(2)}) collective-permute-start(f32[16,6144]{1,0:T(8,128)S(1)} %pad_maximum_fusion.1), channel_id=1, source_target_pairs={{0,8},{4,20},{8,0},{12,28},{16,24},{20,4},{24,16},{28,12},{1,9},{5... | collective-permute-start | bytes 1179656 | tf_op jit(solution)/shard_map/ppermute | solution.py:132
  68.4 10.9 %collective-permute-start.19 = (f32[32,6144]{1,0:T(8,128)S(1)}, f32[32,6144]{1,0:T(8,128)S(1)}, u32[]{:S(2)}, u32[]{:S(2)}) collective-permute-start(f32[32,6144]{1,0:T(8,128)S(1)} %collective-permute-done.15.refs_9_), channel_id=1, source_target_pairs={{0,4},{4,0},{8,12},{12,8},{16,20},{20,16},{24,28},{28,24},{1,5},{5... | collective-permute-start | bytes 2359304 | tf_op jit(solution)/shard_map/ppermute | solution.py:132
  79.0 14.7 %collective-permute-start.16 = (f32[32,6144]{1,0:T(8,128)S(1)}, f32[32,6144]{1,0:T(8,128)S(1)}, u32[]{:S(2)}, u32[]{:S(2)}) collective-permute-start(f32[32,6144]{1,0:T(8,128)S(1)} %constant_dynamic-update-slice_fusion.2.refs_8_), channel_id=1, source_target_pairs={{0,16},{4,12},{8,24},{12,4},{16,0},{20,28},{24,8},{28,20},{1,17},{... | collective-permute-start | bytes 2359304 | tf_op jit(solution)/shard_map/ppermute | solution.py:132
  79.3 15.4 %collective-permute-start.17 = (f32[32,6144]{1,0:T(8,128)S(1)}, f32[32,6144]{1,0:T(8,128)S(1)}, u32[]{:S(2)}, u32[]{:S(2)}) collective-permute-start(f32[32,6144]{1,0:T(8,128)S(1)} %constant_dynamic-update-slice_fusion.2.refs_8_), channel_id=1, source_target_pairs={{0,4},{4,0},{8,12},{12,8},{16,20},{20,16},{24,28},{28,24},{1,5},{5... | collective-permute-start | bytes 2359304 | tf_op jit(solution)/shard_map/ppermute | solution.py:132
  79.3 13.4 %collective-permute-start.22 = (f32[16,4096]{1,0:T(8,128)S(1)}, f32[16,4096]{1,0:T(8,128)S(1)}, u32[]{:S(2)}, u32[]{:S(2)}) collective-permute-start(f32[16,4096]{1,0:T(8,128)S(1)} %pad_maximum_fusion.3), channel_id=1, source_target_pairs={{0,8},{4,20},{8,0},{12,28},{16,24},{20,4},{24,16},{28,12},{1,9},{5... | collective-permute-start | bytes 786440 | tf_op jit(solution)/shard_map/ppermute | solution.py:132
  93.8 14.0 %collective-permute-start.24 = (f32[32,4096]{1,0:T(8,128)S(1)}, f32[32,4096]{1,0:T(8,128)S(1)}, u32[]{:S(2)}, u32[]{:S(2)}) collective-permute-start(f32[32,4096]{1,0:T(8,128)S(1)} %constant_dynamic-update-slice_fusion.8.refs_0_), channel_id=1, source_target_pairs={{0,16},{4,12},{8,24},{12,4},{16,0},{20,28},{24,8},{28,20},{1,17},{... | collective-permute-start | bytes 1572872 | tf_op jit(solution)/shard_map/ppermute | solution.py:132
  94.3 18.4 %collective-permute-start.25 = (f32[32,4096]{1,0:T(8,128)S(1)}, f32[32,4096]{1,0:T(8,128)S(1)}, u32[]{:S(2)}, u32[]{:S(2)}) collective-permute-start(f32[32,4096]{1,0:T(8,128)S(1)} %constant_dynamic-update-slice_fusion.8.refs_0_), channel_id=1, source_target_pairs={{0,4},{4,0},{8,12},{12,8},{16,20},{20,16},{24,28},{28,24},{1,5},{5... | collective-permute-start | bytes 1572872 | tf_op jit(solution)/shard_map/ppermute | solution.py:132
  112.8 12.4 %collective-permute-start.28 = (f32[32,768]{1,0:T(8,128)S(1)}, f32[32,768]{1,0:T(8,128)S(1)}, u32[]{:S(2)}, u32[]{:S(2)}) collective-permute-start(f32[32,768]{1,0:T(8,128)S(1)} %get-tuple-element.54), channel_id=1, source_target_pairs={{0,3},{1,2},{2,1},{3,0},{4,7},{5,6},{6,5},{7,4},{8,11},{9,10},{10,... | collective-permute-start | bytes 294920 | tf_op jit(solution)/shard_map/ppermute | solution.py:132
  120.8 10.3 %collective-permute-start.31 = (f32[32,768]{1,0:T(8,128)S(1)}, f32[32,768]{1,0:T(8,128)S(1)}, u32[]{:S(2)}, u32[]{:S(2)}) collective-permute-start(f32[32,768]{1,0:T(8,128)S(1)} %get-tuple-element.57), channel_id=1, source_target_pairs={{0,2},{1,3},{2,0},{3,1},{4,6},{5,7},{6,4},{7,5},{8,10},{9,11},{10,... | collective-permute-start | bytes 294920 | tf_op jit(solution)/shard_map/ppermute | solution.py:132
  (13 other events, 105.4 us)

commit v4 on v3

--- a/solution.py
+++ b/solution.py
@@ -12,7 +12,7 @@
 SUB, LANE, MXU = 8, 128, 256
 
 PARTS = (3, 3, 2)
-TILE, LIMIT = 2048, 22
+TILE, STEP, LIMIT = 2048, 2048, 22
 COST = 3
 
 
@@ -174,7 +174,7 @@
         last = begin + width == block
         v = held.get(begin)
         acc = multiply(
-            where, integrals if v is None else v, quads, totals[halves[0]], begin, width, TILE, lanes, last, v is not None
+            where, integrals if v is None else v, quads, totals[halves[0]], begin, width, STEP if v is None else TILE, lanes, last, v is not None
         )
         for place, half in enumerate(halves):
             totals[half] = (acc, place)
@@ -187,6 +187,7 @@
         sums[half] = [mine(col)] + [send(mine(col ^ d), "col", xor(cols, d)) for d in range(1, cols)]
 
     piece[0] = cut(0, 0, block)
+    tau = lax.optimization_barrier((tau, piece[0]))[0]
     to_near(0)
     along(1)
     seen.append(first[0])

time: 132 us -> 132 us (level)
    dynamic_slice x3 -> x4, local copies, waits for them, and re-layouts: 2.29 us -> 3.16 us  [cut(): lax.dynamic_slice(tau, (0, (col ^ d) * block + begin), (lanes, width))]
where the time goes in v4:
time: 132 us; the launch traced here: 131 us
  starting transfers between devices  43.6 us (33%)
  waiting for transfers between devices  40.2 us (30%)
  Pallas kernels  31.7 us (24%)
  local copies, waits for them, and re-layouts  14.1 us (11%)
  other arithmetic  1.34 us (1%)
    ppermute x33, starting transfers between devices, send(): return lax.ppermute(lax.optimization_barrier((x, *seen))[0], axis, pairs)  43.6 us
    ppermute x33, waiting for transfers between devices, send(): return lax.ppermute(lax.optimization_barrier((x, *seen))[0], axis, pairs)  40.2 us
    pallas_call x4, Pallas kernels, multiply(): pl.pallas_call(functools.partial(kernel, groups=groups, lanes=lanes, acc=...  31.7 us
    slice x1, local copies, waits for them, and re-layouts, hold(): v = lax.slice(v, (0, begin), (height, begin + parts[u - 2]))  9.95 us
    dynamic_slice x4, local copies, waits for them, and re-layouts, cut(): lax.dynamic_slice(tau, (0, (col ^ d) * block + begin), (lanes, width))  3.16 us
  transfers between devices with their start and end apart: 33, of which 14 were waited for; matrix products, arithmetic and copies ran while one was open for 9% of the time, Pallas kernels for 24%

profile of v4, /device:TPU:0, one launch (start us, length us, event | category | flops | bytes accessed | tf_op | source)
XLA Modules:
  0.0 131.3 jit_solution(3301822817705578997)
XLA Ops:
  1.2 1.9 %constant_dynamic-slice_fusion.14 = f32[8,16384]{1,0:T(8,128)} fusion(f32[8,65536]{1,0:T(8,128)} %bitcast.18, s32[]{:T(128)S(6)} %select_n.106), kind=kLoop, calls=%fused_computation.56 | loop fusion | bytes 1048580 | tf_op jit(solution)/shard_map/dynamic_slice | solution.py:135
  3.1 3.0 %collective-permute-start.1 = (f32[8,16384]{1,0:T(8,128)}, f32[8,16384]{1,0:T(8,128)S(1)}, u32[]{:S(2)}, u32[]{:S(2)}) collective-permute-start(f32[8,16384]{1,0:T(8,128)} %constant_dynamic-slice_fusion.14), channel_id=1, source_target_pairs={{0,1},{1,0},{2,3},{3,2},{4,5},{5,4},{6,7},{7,6},{8,9},{9,8},{10,11... | collective-permute-start | bytes 1572872 | tf_op jit(solution)/shard_map/ppermute | solution.py:132
  7.8 7.6 %collective-permute-done = f32[8,16384]{1,0:T(8,128)} collective-permute-done((f32[8,16384]{1,0:T(8,128)S(1)}, f32[8,16384]{1,0:T(8,128)}, u32[]{:S(2)}, u32[]{:S(2)}) %collective-permute-start) | collective-permute-done | bytes 524320 | tf_op jit(solution)/shard_map/ppermute | solution.py:132
  16.5 1.6 %collective-permute-start.2 = (f32[16,16384]{1,0:T(8,128)S(1)}, f32[16,16384]{1,0:T(8,128)S(1)}, u32[]{:S(2)}, u32[]{:S(2)}) collective-permute-start(f32[16,16384]{1,0:T(8,128)S(1)} %pad_maximum_fusion.refs_0_), channel_id=1, source_target_pairs={{0,16},{4,12},{8,24},{12,4},{16,0},{20,28},{24,8},{28,20},{1,17},{... | collective-permute-start | bytes 3145736 | tf_op jit(solution)/shard_map/ppermute | solution.py:132
  18.3 1.7 %collective-permute-start.5 = (f32[8,16384]{1,0:T(8,128)S(1)}, f32[8,16384]{1,0:T(8,128)S(1)}, u32[]{:S(2)}, u32[]{:S(2)}) collective-permute-start(f32[8,16384]{1,0:T(8,128)S(1)} %collective-permute-done.1), channel_id=1, source_target_pairs={{0,8},{4,20},{8,0},{12,28},{16,24},{20,4},{24,16},{28,12},{1,9},{5... | collective-permute-start | bytes 1572872 | tf_op jit(solution)/shard_map/ppermute | solution.py:132
  19.9 2.6 %collective-permute-start.8 = (f32[8,6144]{1,0:T(8,128)S(1)}, f32[8,6144]{1,0:T(8,128)S(1)}, u32[]{:S(2)}, u32[]{:S(2)}) collective-permute-start(f32[8,6144]{1,0:T(8,128)S(1)} %get-tuple-element.39), channel_id=1, source_target_pairs={{0,2},{1,3},{2,0},{3,1},{4,6},{5,7},{6,4},{7,5},{8,10},{9,11},{10,... | collective-permute-start | bytes 589832 | tf_op jit(solution)/shard_map/ppermute | solution.py:132
  23.9 10.0 %slice.54.v_ref = f32[704,4096]{1,0:T(8,128)} slice(f32[704,16384]{1,0:T(8,128)} %v_ref.3), slice={[0:704], [12288:16384]} | slice | bytes 23068672 | tf_op jit(solution)/shard_map/slice | solution.py:163
  33.9 2.1 %collective-permute-done.8 = f32[8,6144]{1,0:T(8,128)S(1)} collective-permute-done((f32[8,6144]{1,0:T(8,128)S(1)}, f32[8,6144]{1,0:T(8,128)S(1)}, u32[]{:S(2)}, u32[]{:S(2)}) %collective-permute-start.8) | collective-permute-done | bytes 196640 | tf_op jit(solution)/shard_map/ppermute | solution.py:132
  40.2 4.3 %collective-permute-start.11 = (f32[8,6144]{1,0:T(8,128)S(1)}, f32[8,6144]{1,0:T(8,128)S(1)}, u32[]{:S(2)}, u32[]{:S(2)}) collective-permute-start(f32[8,6144]{1,0:T(8,128)S(1)} %get-tuple-element.42), channel_id=1, source_target_pairs={{0,2},{1,3},{2,0},{3,1},{4,6},{5,7},{6,4},{7,5},{8,10},{9,11},{10,... | collective-permute-start | bytes 589832 | tf_op jit(solution)/shard_map/ppermute | solution.py:132
  44.5 6.2 %collective-permute-done.13 = f32[16,6144]{1,0:T(8,128)S(1)} collective-permute-done((f32[16,6144]{1,0:T(8,128)S(1)}, f32[16,6144]{1,0:T(8,128)S(1)}, u32[]{:S(2)}, u32[]{:S(2)}) %collective-permute-start.13) | collective-permute-done | bytes 393248 | tf_op jit(solution)/shard_map/ppermute | solution.py:132
  50.7 2.5 %collective-permute-start.12 = (f32[8,6144]{1,0:T(8,128)S(1)}, f32[8,6144]{1,0:T(8,128)S(1)}, u32[]{:S(2)}, u32[]{:S(2)}) collective-permute-start(f32[8,6144]{1,0:T(8,128)S(1)} %get-tuple-element.43), channel_id=1, source_target_pairs={{0,3},{1,2},{2,1},{3,0},{4,7},{5,6},{6,5},{7,4},{8,11},{9,10},{10,... | collective-permute-start | bytes 589832 | tf_op jit(solution)/shard_map/ppermute | solution.py:132
  53.2 2.9 %collective-permute-done.6.refs_5_ = f32[16,16384]{1,0:T(8,128)S(1)} collective-permute-done((f32[16,16384]{1,0:T(8,128)S(1)}, f32[16,16384]{1,0:T(8,128)S(1)}, u32[]{:S(2)}, u32[]{:S(2)}) %collective-permute-start.6) | collective-permute-done | bytes 1048608 | tf_op jit(solution)/shard_map/ppermute | solution.py:132
  58.7 2.7 %collective-permute-done.10.refs_7_ = f32[16,16384]{1,0:T(8,128)S(1)} collective-permute-done((f32[16,16384]{1,0:T(8,128)S(1)}, f32[16,16384]{1,0:T(8,128)S(1)}, u32[]{:S(2)}, u32[]{:S(2)}) %collective-permute-start.10) | collective-permute-done | bytes 1048608 | tf_op jit(solution)/shard_map/ppermute | solution.py:132
  61.4 2.5 %collective-permute-start.21 = (f32[8,4096]{1,0:T(8,128)S(1)}, f32[8,4096]{1,0:T(8,128)S(1)}, u32[]{:S(2)}, u32[]{:S(2)}) collective-permute-start(f32[8,4096]{1,0:T(8,128)S(1)} %get-tuple-element.50), channel_id=1, source_target_pairs={{0,3},{1,2},{2,1},{3,0},{4,7},{5,6},{6,5},{7,4},{8,11},{9,10},{10,... | collective-permute-start | bytes 393224 | tf_op jit(solution)/shard_map/ppermute | solution.py:132
  63.9 3.5 %collective-permute-start.20 = (f32[8,4096]{1,0:T(8,128)S(1)}, f32[8,4096]{1,0:T(8,128)S(1)}, u32[]{:S(2)}, u32[]{:S(2)}) collective-permute-start(f32[8,4096]{1,0:T(8,128)S(1)} %get-tuple-element.49), channel_id=1, source_target_pairs={{0,2},{1,3},{2,0},{3,1},{4,6},{5,7},{6,4},{7,5},{8,10},{9,11},{10,... | collective-permute-start | bytes 393224 | tf_op jit(solution)/shard_map/ppermute | solution.py:132
  68.8 8.4 %collective-permute-done.20 = f32[8,4096]{1,0:T(8,128)S(1)} collective-permute-done((f32[8,4096]{1,0:T(8,128)S(1)}, f32[8,4096]{1,0:T(8,128)S(1)}, u32[]{:S(2)}, u32[]{:S(2)}) %collective-permute-start.20) | collective-permute-done | bytes 131104 | tf_op jit(solution)/shard_map/ppermute | solution.py:132
  79.8 11.4 %shard_map.28.refs_12_ = f32[704,256]{1,0:T(8,128)S(1)} custom-call(s32[2]{0:T(128)S(1)} %pad_add_fusion.where, f32[704,16384]{1,0:T(8,128)} %v_ref.3, f32[16,16384]{1,0:T(8,128)S(1)} %pad_maximum_fusion.refs_0_, f32[16,16384]{1,0:T(8,128)S(1)} %collective-permute-done.2.refs_1_, f32[16,16384]{1,0:T(8,128)S(1)} %collective-permute-done.3.refs_2_, ...), custom_call_target="tpu_custom_call" | custom-call | flops 19931332608 | bytes 70778880 | tf_op jit(solution)/shard_map/pallas_call | solution.py:99
  94.6 11.6 %shard_map.29.refs_8_.refs_4_ = f32[704,256]{1,0:T(8,128)S(1)} custom-call(s32[2]{0:T(128)S(1)} %pad_add_fusion.where, f32[704,16384]{1,0:T(8,128)} %v_ref.3, f32[16,16384]{1,0:T(8,128)S(1)} %pad_maximum_fusion.refs_0_, f32[16,16384]{1,0:T(8,128)S(1)} %collective-permute-done.2.refs_1_, f32[16,16384]{1,0:T(8,128)S(1)} %collective-permute-done.3.refs_2_, ...), custom_call_target="tpu_custom_call" | custom-call | flops 19931332608 | bytes 70778880 | tf_op jit(solution)/shard_map/pallas_call | solution.py:99
  106.7 4.4 %shard_map.30 = f32[128,768]{1,0:T(8,128)S(1)} custom-call(s32[2]{0:T(128)S(1)} %pad_add_fusion.where, f32[704,4096]{1,0:T(8,128)S(1)} %bitcast.17, f32[16,16384]{1,0:T(8,128)S(1)} %pad_maximum_fusion.refs_0_, f32[16,16384]{1,0:T(8,128)S(1)} %collective-permute-done.2.refs_1_, f32[16,16384]{1,0:T(8,128)S(1)} %collective-permute-done.3.refs_2_, ...), custom_call_target="tpu_custom_call" | custom-call | flops 6643777536 | bytes 40894464 | tf_op jit(solution)/shard_map/pallas_call | solution.py:99
  111.2 2.5 %collective-permute-start.28 = (f32[32,768]{1,0:T(8,128)S(1)}, f32[32,768]{1,0:T(8,128)S(1)}, u32[]{:S(2)}, u32[]{:S(2)}) collective-permute-start(f32[32,768]{1,0:T(8,128)S(1)} %get-tuple-element.56), channel_id=1, source_target_pairs={{0,3},{1,2},{2,1},{3,0},{4,7},{5,6},{6,5},{7,4},{8,11},{9,10},{10,... | collective-permute-start | bytes 294920 | tf_op jit(solution)/shard_map/ppermute | solution.py:132
  113.7 4.4 %shard_map.31 = f32[128,768]{1,0:T(8,128)S(1)} custom-call(s32[2]{0:T(128)S(1)} %pad_add_fusion.where, f32[704,4096]{1,0:T(8,128)S(1)} %bitcast.17, f32[32,4096]{1,0:T(8,128)S(1)} %constant_dynamic-update-slice_fusion.8.refs_0_, f32[32,4096]{1,0:T(8,128)S(1)} %collective-permute-done.24.refs_1_, f32[32,4096]{1,0:T(8,128)S(1)} %collective-permute-done.25.refs_2_, ...), custom_call_target="tpu_custom_call" | custom-call | flops 6643777536 | bytes 40894464 | tf_op jit(solution)/shard_map/pallas_call | solution.py:99
  120.2 1.9 %collective-permute-start.31 = (f32[32,768]{1,0:T(8,128)S(1)}, f32[32,768]{1,0:T(8,128)S(1)}, u32[]{:S(2)}, u32[]{:S(2)}) collective-permute-start(f32[32,768]{1,0:T(8,128)S(1)} %get-tuple-element.59), channel_id=1, source_target_pairs={{0,2},{1,3},{2,0},{3,1},{4,6},{5,7},{6,4},{7,5},{8,10},{9,11},{10,... | collective-permute-start | bytes 294920 | tf_op jit(solution)/shard_map/ppermute | solution.py:132
  125.0 1.7 %collective-permute-done.30 = f32[32,768]{1,0:T(8,128)S(1)} collective-permute-done((f32[32,768]{1,0:T(8,128)S(1)}, f32[32,768]{1,0:T(8,128)S(1)}, u32[]{:S(2)}, u32[]{:S(2)}) %collective-permute-start.30) | collective-permute-done | bytes 98336 | tf_op jit(solution)/shard_map/ppermute | solution.py:132
  126.7 3.8 %collective-permute-done.31 = f32[32,768]{1,0:T(8,128)S(1)} collective-permute-done((f32[32,768]{1,0:T(8,128)S(1)}, f32[32,768]{1,0:T(8,128)S(1)}, u32[]{:S(2)}, u32[]{:S(2)}) %collective-permute-start.31) | collective-permute-done | bytes 98336 | tf_op jit(solution)/shard_map/ppermute | solution.py:132
  (82 shorter events, 26.0 us)
Async XLA Ops:
  3.1 15.2 %collective-permute-start.1 = (f32[8,16384]{1,0:T(8,128)}, f32[8,16384]{1,0:T(8,128)S(1)}, u32[]{:S(2)}, u32[]{:S(2)}) collective-permute-start(f32[8,16384]{1,0:T(8,128)} %constant_dynamic-slice_fusion.14), channel_id=1, source_target_pairs={{0,1},{1,0},{2,3},{3,2},{4,5},{5,4},{6,7},{7,6},{8,9},{9,8},{10,11... | collective-permute-start | bytes 1572872 | tf_op jit(solution)/shard_map/ppermute | solution.py:132
  6.1 9.3 %collective-permute-start = (f32[8,16384]{1,0:T(8,128)S(1)}, f32[8,16384]{1,0:T(8,128)}, u32[]{:S(2)}, u32[]{:S(2)}) collective-permute-start(f32[8,16384]{1,0:T(8,128)S(1)} %dynamic-slice_bitcast_fusion), channel_id=1, source_target_pairs={{0,8},{4,20},{8,0},{12,28},{16,24},{20,4},{24,16},{28,12},{1,9},{5... | collective-permute-start | bytes 1572872 | tf_op jit(solution)/shard_map/ppermute | solution.py:132
  16.5 20.5 %collective-permute-start.2 = (f32[16,16384]{1,0:T(8,128)S(1)}, f32[16,16384]{1,0:T(8,128)S(1)}, u32[]{:S(2)}, u32[]{:S(2)}) collective-permute-start(f32[16,16384]{1,0:T(8,128)S(1)} %pad_maximum_fusion.refs_0_), channel_id=1, source_target_pairs={{0,16},{4,12},{8,24},{12,4},{16,0},{20,28},{24,8},{28,20},{1,17},{... | collective-permute-start | bytes 3145736 | tf_op jit(solution)/shard_map/ppermute | solution.py:132
  18.1 40.6 %collective-permute-start.3 = (f32[16,16384]{1,0:T(8,128)S(1)}, f32[16,16384]{1,0:T(8,128)S(1)}, u32[]{:S(2)}, u32[]{:S(2)}) collective-permute-start(f32[16,16384]{1,0:T(8,128)S(1)} %pad_maximum_fusion.refs_0_), channel_id=1, source_target_pairs={{0,4},{4,0},{8,12},{12,8},{16,20},{20,16},{24,28},{28,24},{1,5},{5... | collective-permute-start | bytes 3145736 | tf_op jit(solution)/shard_map/ppermute | solution.py:132
  18.3 17.7 %collective-permute-start.5 = (f32[8,16384]{1,0:T(8,128)S(1)}, f32[8,16384]{1,0:T(8,128)S(1)}, u32[]{:S(2)}, u32[]{:S(2)}) collective-permute-start(f32[8,16384]{1,0:T(8,128)S(1)} %collective-permute-done.1), channel_id=1, source_target_pairs={{0,8},{4,20},{8,0},{12,28},{16,24},{20,4},{24,16},{28,12},{1,9},{5... | collective-permute-start | bytes 1572872 | tf_op jit(solution)/shard_map/ppermute | solution.py:132
  19.9 16.0 %collective-permute-start.8 = (f32[8,6144]{1,0:T(8,128)S(1)}, f32[8,6144]{1,0:T(8,128)S(1)}, u32[]{:S(2)}, u32[]{:S(2)}) collective-permute-start(f32[8,6144]{1,0:T(8,128)S(1)} %get-tuple-element.39), channel_id=1, source_target_pairs={{0,2},{1,3},{2,0},{3,1},{4,6},{5,7},{6,4},{7,5},{8,10},{9,11},{10,... | collective-permute-start | bytes 589832 | tf_op jit(solution)/shard_map/ppermute | solution.py:132
  22.5 13.4 %collective-permute-start.9 = (f32[8,6144]{1,0:T(8,128)S(1)}, f32[8,6144]{1,0:T(8,128)S(1)}, u32[]{:S(2)}, u32[]{:S(2)}) collective-permute-start(f32[8,6144]{1,0:T(8,128)S(1)} %get-tuple-element.40), channel_id=1, source_target_pairs={{0,3},{1,2},{2,1},{3,0},{4,7},{5,6},{6,5},{7,4},{8,11},{9,10},{10,... | collective-permute-start | bytes 589832 | tf_op jit(solution)/shard_map/ppermute | solution.py:132
  37.0 19.1 %collective-permute-start.6 = (f32[16,16384]{1,0:T(8,128)S(1)}, f32[16,16384]{1,0:T(8,128)S(1)}, u32[]{:S(2)}, u32[]{:S(2)}) collective-permute-start(f32[16,16384]{1,0:T(8,128)S(1)} %constant_dynamic-update-slice_fusion.refs_4_), channel_id=1, source_target_pairs={{0,16},{4,12},{8,24},{12,4},{16,0},{20,28},{24,8},{28,20},{1,17},{... | collective-permute-start | bytes 3145736 | tf_op jit(solution)/shard_map/ppermute | solution.py:132
  38.6 12.1 %collective-permute-start.13 = (f32[16,6144]{1,0:T(8,128)S(1)}, f32[16,6144]{1,0:T(8,128)S(1)}, u32[]{:S(2)}, u32[]{:S(2)}) collective-permute-start(f32[16,6144]{1,0:T(8,128)S(1)} %pad_maximum_fusion.2), channel_id=1, source_target_pairs={{0,8},{4,20},{8,0},{12,28},{16,24},{20,4},{24,16},{28,12},{1,9},{5... | collective-permute-start | bytes 1179656 | tf_op jit(solution)/shard_map/ppermute | solution.py:132
  40.1 18.6 %collective-permute-start.4 = (f32[16,16384]{1,0:T(8,128)S(1)}, f32[16,16384]{1,0:T(8,128)S(1)}, u32[]{:S(2)}, u32[]{:S(2)}) collective-permute-start(f32[16,16384]{1,0:T(8,128)S(1)} %collective-permute-done.2.refs_1_), channel_id=1, source_target_pairs={{0,4},{4,0},{8,12},{12,8},{16,20},{20,16},{24,28},{28,24},{1,5},{5... | collective-permute-start | bytes 3145736 | tf_op jit(solution)/shard_map/ppermute | solution.py:132
  40.2 17.4 %collective-permute-start.11 = (f32[8,6144]{1,0:T(8,128)S(1)}, f32[8,6144]{1,0:T(8,128)S(1)}, u32[]{:S(2)}, u32[]{:S(2)}) collective-permute-start(f32[8,6144]{1,0:T(8,128)S(1)} %get-tuple-element.42), channel_id=1, source_target_pairs={{0,2},{1,3},{2,0},{3,1},{4,6},{5,7},{6,4},{7,5},{8,10},{9,11},{10,... | collective-permute-start | bytes 589832 | tf_op jit(solution)/shard_map/ppermute | solution.py:132
  56.1 12.5 %collective-permute-start.15 = (f32[32,6144]{1,0:T(8,128)S(1)}, f32[32,6144]{1,0:T(8,128)S(1)}, u32[]{:S(2)}, u32[]{:S(2)}) collective-permute-start(f32[32,6144]{1,0:T(8,128)S(1)} %constant_dynamic-update-slice_fusion.5.refs_8_), channel_id=1, source_target_pairs={{0,16},{4,12},{8,24},{12,4},{16,0},{20,28},{24,8},{28,20},{1,17},{... | collective-permute-start | bytes 2359304 | tf_op jit(solution)/shard_map/ppermute | solution.py:132
  57.6 21.7 %collective-permute-start.18 = (f32[32,6144]{1,0:T(8,128)S(1)}, f32[32,6144]{1,0:T(8,128)S(1)}, u32[]{:S(2)}, u32[]{:S(2)}) collective-permute-start(f32[32,6144]{1,0:T(8,128)S(1)} %constant_dynamic-update-slice_fusion.5.refs_8_), channel_id=1, source_target_pairs={{0,4},{4,0},{8,12},{12,8},{16,20},{20,16},{24,28},{28,24},{1,5},{5... | collective-permute-start | bytes 2359304 | tf_op jit(solution)/shard_map/ppermute | solution.py:132
  63.9 13.3 %collective-permute-start.20 = (f32[8,4096]{1,0:T(8,128)S(1)}, f32[8,4096]{1,0:T(8,128)S(1)}, u32[]{:S(2)}, u32[]{:S(2)}) collective-permute-start(f32[8,4096]{1,0:T(8,128)S(1)} %get-tuple-element.49), channel_id=1, source_target_pairs={{0,2},{1,3},{2,0},{3,1},{4,6},{5,7},{6,4},{7,5},{8,10},{9,11},{10,... | collective-permute-start | bytes 393224 | tf_op jit(solution)/shard_map/ppermute | solution.py:132
  67.4 9.8 %collective-permute-start.14 = (f32[16,6144]{1,0:T(8,128)S(1)}, f32[16,6144]{1,0:T(8,128)S(1)}, u32[]{:S(2)}, u32[]{:S(2)}) collective-permute-start(f32[16,6144]{1,0:T(8,128)S(1)} %pad_maximum_fusion.1), channel_id=1, source_target_pairs={{0,8},{4,20},{8,0},{12,28},{16,24},{20,4},{24,16},{28,12},{1,9},{5... | collective-permute-start | bytes 1179656 | tf_op jit(solution)/shard_map/ppermute | solution.py:132
  68.6 10.7 %collective-permute-start.19 = (f32[32,6144]{1,0:T(8,128)S(1)}, f32[32,6144]{1,0:T(8,128)S(1)}, u32[]{:S(2)}, u32[]{:S(2)}) collective-permute-start(f32[32,6144]{1,0:T(8,128)S(1)} %collective-permute-done.15.refs_9_), channel_id=1, source_target_pairs={{0,4},{4,0},{8,12},{12,8},{16,20},{20,16},{24,28},{28,24},{1,5},{5... | collective-permute-start | bytes 2359304 | tf_op jit(solution)/shard_map/ppermute | solution.py:132
  77.3 14.9 %collective-permute-start.16 = (f32[32,6144]{1,0:T(8,128)S(1)}, f32[32,6144]{1,0:T(8,128)S(1)}, u32[]{:S(2)}, u32[]{:S(2)}) collective-permute-start(f32[32,6144]{1,0:T(8,128)S(1)} %constant_dynamic-update-slice_fusion.2.refs_8_), channel_id=1, source_target_pairs={{0,16},{4,12},{8,24},{12,4},{16,0},{20,28},{24,8},{28,20},{1,17},{... | collective-permute-start | bytes 2359304 | tf_op jit(solution)/shard_map/ppermute | solution.py:132
  78.7 15.9 %collective-permute-start.17 = (f32[32,6144]{1,0:T(8,128)S(1)}, f32[32,6144]{1,0:T(8,128)S(1)}, u32[]{:S(2)}, u32[]{:S(2)}) collective-permute-start(f32[32,6144]{1,0:T(8,128)S(1)} %constant_dynamic-update-slice_fusion.2.refs_8_), channel_id=1, source_target_pairs={{0,4},{4,0},{8,12},{12,8},{16,20},{20,16},{24,28},{28,24},{1,5},{5... | collective-permute-start | bytes 2359304 | tf_op jit(solution)/shard_map/ppermute | solution.py:132
  79.3 11.8 %collective-permute-start.22 = (f32[16,4096]{1,0:T(8,128)S(1)}, f32[16,4096]{1,0:T(8,128)S(1)}, u32[]{:S(2)}, u32[]{:S(2)}) collective-permute-start(f32[16,4096]{1,0:T(8,128)S(1)} %pad_maximum_fusion.3), channel_id=1, source_target_pairs={{0,8},{4,20},{8,0},{12,28},{16,24},{20,4},{24,16},{28,12},{1,9},{5... | collective-permute-start | bytes 786440 | tf_op jit(solution)/shard_map/ppermute | solution.py:132
  92.2 14.0 %collective-permute-start.24 = (f32[32,4096]{1,0:T(8,128)S(1)}, f32[32,4096]{1,0:T(8,128)S(1)}, u32[]{:S(2)}, u32[]{:S(2)}) collective-permute-start(f32[32,4096]{1,0:T(8,128)S(1)} %constant_dynamic-update-slice_fusion.8.refs_0_), channel_id=1, source_target_pairs={{0,16},{4,12},{8,24},{12,4},{16,0},{20,28},{24,8},{28,20},{1,17},{... | collective-permute-start | bytes 1572872 | tf_op jit(solution)/shard_map/ppermute | solution.py:132
  93.7 17.4 %collective-permute-start.25 = (f32[32,4096]{1,0:T(8,128)S(1)}, f32[32,4096]{1,0:T(8,128)S(1)}, u32[]{:S(2)}, u32[]{:S(2)}) collective-permute-start(f32[32,4096]{1,0:T(8,128)S(1)} %constant_dynamic-update-slice_fusion.8.refs_0_), channel_id=1, source_target_pairs={{0,4},{4,0},{8,12},{12,8},{16,20},{20,16},{24,28},{28,24},{1,5},{5... | collective-permute-start | bytes 1572872 | tf_op jit(solution)/shard_map/ppermute | solution.py:132
  111.1 11.0 %collective-permute-start.27 = (f32[32,768]{1,0:T(8,128)S(1)}, f32[32,768]{1,0:T(8,128)S(1)}, u32[]{:S(2)}, u32[]{:S(2)}) collective-permute-start(f32[32,768]{1,0:T(8,128)S(1)} %get-tuple-element.55), channel_id=1, source_target_pairs={{0,2},{1,3},{2,0},{3,1},{4,6},{5,7},{6,4},{7,5},{8,10},{9,11},{10,... | collective-permute-start | bytes 294920 | tf_op jit(solution)/shard_map/ppermute | solution.py:132
  111.2 12.4 %collective-permute-start.28 = (f32[32,768]{1,0:T(8,128)S(1)}, f32[32,768]{1,0:T(8,128)S(1)}, u32[]{:S(2)}, u32[]{:S(2)}) collective-permute-start(f32[32,768]{1,0:T(8,128)S(1)} %get-tuple-element.56), channel_id=1, source_target_pairs={{0,3},{1,2},{2,1},{3,0},{4,7},{5,6},{6,5},{7,4},{8,11},{9,10},{10,... | collective-permute-start | bytes 294920 | tf_op jit(solution)/shard_map/ppermute | solution.py:132
  120.2 10.2 %collective-permute-start.31 = (f32[32,768]{1,0:T(8,128)S(1)}, f32[32,768]{1,0:T(8,128)S(1)}, u32[]{:S(2)}, u32[]{:S(2)}) collective-permute-start(f32[32,768]{1,0:T(8,128)S(1)} %get-tuple-element.59), channel_id=1, source_target_pairs={{0,2},{1,3},{2,0},{3,1},{4,6},{5,7},{6,4},{7,5},{8,10},{9,11},{10,... | collective-permute-start | bytes 294920 | tf_op jit(solution)/shard_map/ppermute | solution.py:132
  (13 other events, 102.4 us)
